TPU v7x, 256 devices: a whole 4x4x8 slice. The times are simulated.
256 devices in a mesh: pa: 16 (over z_hi, y, core), pb: 16 (over x, z_lo).
Axes of the slice: x: 4, y: 4, z: 8 (z_hi: 2, z_lo: 4; z = z_hi * 4 + z_lo), core: 2. Of those that a mesh axis runs over, the one named last changes fastest.
Arguments:
- field: float32 [16, 64, 256, 256], P(None, 'pa', 'pb'), may hold values from -600 to 600
- spline_index: int32 [16, 64, 256, 256], P(None, 'pa', 'pb'), may hold values from 0 to 4
- spec_weight: float32 [2, 16, 16, 32, 32, 16], P(None, None, None, None, 'pa', 'pb'), may hold values from -6 to 6
- local_weight: float32 [16, 16], replicated, may hold values from -1.5 to 1.5
- bn_gain: float32 [16], replicated, may hold values from 0.1 to 1.9
- bn_shift: float32 [16], replicated, may hold values from -3 to 3
- base_weight: float32 [16, 16], replicated, may hold values from -1.5 to 1.5
- spline_coef: float32 [16, 16, 8], replicated, may hold values from -0.75 to 0.75
Outputs:
- output: float32 [16, 64, 256, 256], P(None, 'pa', 'pb')
All inputs are finite; a program needn't handle non-finite values.
Results may differ from a plain program's by a relative error of at most 0.0003.
Values sent between devices are 32-bit elements; how exact they have to be, the bound alone decides.
No kernel may reach another device: no remote copies, remote signals or barrier semaphores. Data moves between devices by JAX's collectives and lax.ppermute only.
A program may use at most 128 MiB of HBM per device.

v0:
```python
import jax
import jax.numpy as jnp
import numpy as np
from jax import lax
from jax.sharding import PartitionSpec as P

NZ = 64
NX = 256
NY = 256
MZ = 16
MX = 16
MY = 16
INTERVALS = 5
KZ = 32
KX = 32
NB = 8


EPSILON = 1e-05
GRID_RADIUS = 2.0
HIGH = lax.Precision.HIGHEST


def kan_apply(normed, spline_index, base_weight, spline_coef):
    step = 2.0 * GRID_RADIUS / INTERVALS
    left = spline_index.astype(normed.dtype) * step - GRID_RADIUS
    local_coord = jnp.clip((normed - left) / step, 0.0, 1.0)
    complement = 1.0 - local_coord
    cube = local_coord * local_coord * local_coord
    square = local_coord * local_coord
    pieces = [
        complement * complement * complement / 6.0,
        (3.0 * cube - 6.0 * square + 4.0) / 6.0,
        (-3.0 * cube + 3.0 * square + 3.0 * local_coord + 1.0) / 6.0,
        cube / 6.0,
    ]
    zeros = jnp.zeros_like(normed)
    result = jnp.einsum("oi,i...->o...", base_weight, jax.nn.silu(normed), precision=HIGH)
    for basis in range(NB):
        total = zeros
        for offset in range(4):
            total = total + jnp.where(spline_index == basis - offset, pieces[offset], zeros)
        result = result + jnp.einsum(
            "oi,i...->o...", spline_coef[:, :, basis], total, precision=HIGH
        )
    return result


def mode_order(count, lower_kept, upper_kept, groups):
    kept = np.concatenate([np.arange(lower_kept), np.arange(count - upper_kept, count)]).astype(
        np.int64
    )
    others = np.arange(lower_kept, count - upper_kept).astype(np.int64)
    kept_blocks = kept.reshape(groups, -1)
    other_blocks = others.reshape(groups, -1)
    return np.concatenate([kept_blocks, other_blocks], axis=1).reshape(-1)


def dft_tables(length, modes):
    phase = np.arange(length).astype(np.int64)[:, None] * modes[None, :] % length
    angle = phase * (2.0 * np.pi / length)
    return (np.cos(angle), np.sin(angle))


def complex_table(cosine, sine, sign, factor):
    table = np.stack([np.stack([cosine, -sign * sine]), np.stack([sign * sine, cosine])]) * factor
    return jnp.asarray(table, jnp.float32)


def on_device(
    field, spline_index, spec_weight, local_weight, bn_gain, bn_shift, base_weight, spline_coef
):
    groups_a = lax.axis_size("pa")
    groups_b = lax.axis_size("pb")
    y_modes = mode_order(NY // 2, MY, 0, groups_b)
    x_modes = mode_order(NX, MX, MX, groups_a)
    z_modes = mode_order(NZ, MZ, MZ, 1)
    kept_y = MY // groups_b
    kept_x = KX // groups_a
    held_y = y_modes.shape[0] // groups_b
    held_x = x_modes.shape[0] // groups_a
    y_cos, y_sin = dft_tables(NY, y_modes)
    x_cos, x_sin = dft_tables(NX, x_modes)
    z_cos, z_sin = dft_tables(NZ, z_modes)
    twice = np.where(y_modes == 0, 1.0, 2.0) / NY
    y_forward = jnp.asarray(np.stack([y_cos, -y_sin]), jnp.float32)
    y_inverse = jnp.asarray(
        np.stack([y_cos * twice[None, :], -y_sin * twice[None, :]]), jnp.float32
    )
    x_forward = complex_table(x_cos, x_sin, 1.0, 1.0)
    x_inverse = complex_table(x_cos, x_sin, -1.0, 1.0 / NX)
    z_forward = complex_table(z_cos, z_sin, 1.0, 1.0)
    z_inverse = complex_table(z_cos, z_sin, -1.0, 1.0 / NZ)
    spectrum = jnp.einsum("czxy,pyk->pczxk", field, y_forward, precision=HIGH)
    rows = jnp.einsum(
        "qczxy,qpxk->pczky",
        lax.all_to_all(spectrum, "pb", split_axis=4, concat_axis=3, tiled=True),
        x_forward,
        precision=HIGH,
    )
    planes = lax.all_to_all(rows, "pa", split_axis=3, concat_axis=2, tiled=True)
    modes = jnp.einsum("qczxy,qpzk->pckxy", planes, z_forward, precision=HIGH)
    modes_real = modes[0, :, :KZ, :kept_x, :kept_y]
    modes_imag = modes[1, :, :KZ, :kept_x, :kept_y]
    mixed_real = jnp.einsum("iozxy,izxy->ozxy", spec_weight[0], modes_real, precision=HIGH)
    mixed_real = mixed_real - jnp.einsum(
        "iozxy,izxy->ozxy", spec_weight[1], modes_imag, precision=HIGH
    )
    mixed_imag = jnp.einsum("iozxy,izxy->ozxy", spec_weight[0], modes_imag, precision=HIGH)
    mixed_imag = mixed_imag + jnp.einsum(
        "iozxy,izxy->ozxy", spec_weight[1], modes_real, precision=HIGH
    )
    padding = (
        (0, 0),
        (0, 0),
        (0, z_modes.shape[0] - KZ),
        (0, held_x - kept_x),
        (0, held_y - kept_y),
    )
    mixed = jnp.pad(jnp.stack([mixed_real, mixed_imag]), padding)
    backward = jnp.einsum("qckxy,qpzk->pczxy", mixed, z_inverse, precision=HIGH)
    rows_back = jnp.einsum(
        "qczky,qpxk->pczxy",
        lax.all_to_all(backward, "pa", split_axis=2, concat_axis=3, tiled=True),
        x_inverse,
        precision=HIGH,
    )
    spectral = jnp.einsum(
        "qczxk,qyk->czxy",
        lax.all_to_all(rows_back, "pb", split_axis=3, concat_axis=4, tiled=True),
        y_inverse,
        precision=HIGH,
    )
    hidden = spectral + jnp.einsum("oi,izxy->ozxy", local_weight, field, precision=HIGH)
    cells = NZ * NX * NY
    totals = lax.psum(jnp.sum(hidden, axis=(1, 2, 3)), ("pa", "pb"))
    mean = totals / cells
    centered = hidden - mean[:, None, None, None]
    squares = lax.psum(jnp.sum(centered * centered, axis=(1, 2, 3)), ("pa", "pb"))
    var = squares / cells
    scale = bn_gain * lax.rsqrt(var + EPSILON)
    normed = centered * scale[:, None, None, None] + bn_shift[:, None, None, None]

    def slab_step(depth, result):
        piece = lax.dynamic_slice_in_dim(normed, depth, 1, 1)
        index_piece = lax.dynamic_slice_in_dim(spline_index, depth, 1, 1)
        value = kan_apply(piece, index_piece, base_weight, spline_coef)
        return lax.dynamic_update_slice_in_dim(result, value, depth, 1)

    return lax.fori_loop(0, field.shape[1], slab_step, jnp.zeros_like(normed))


def solution(mesh):
    in_specs = (
        P(None, "pa", "pb", None),
        P(None, "pa", "pb", None),
        P(None, None, None, None, "pa", "pb"),
        P(),
        P(),
        P(),
        P(),
        P(),
    )
    out_specs = P(None, "pa", "pb", None)
    return jax.shard_map(
        on_device, mesh=mesh, in_specs=in_specs, out_specs=out_specs, check_vma=False
    )
```

profile of v0, /device:TPU:1, one launch (start us, length us, event | category | flops | bytes accessed | tf_op | source)
XLA Modules:
  0.0 551.2 jit_solution(12577196251125748331)
XLA Ops:
  0.0 1.2 copy-done
  1.2 2.0 convolution_bitcast_fusion.2
  3.2 6.4 %copy.57 = f32[2,16,4,16,128]{3,2,1,0,4:T(4,128)} copy(f32[2,16,4,16,128]{4,3,2,1,0:T(8,128)S(1)} %convolution_bitcast_fusion.2) | data formatting | bytes 2097152 | tf_op jit(solution)/shard_map/czxy,pyk->pczxk/transpose | solution.py:94
  9.6 8.3 %reshape.167 = f32[16,1,16384]{2,1,0:T(1,128)S(1)} reshape(f32[128,2,16,4,16]{4,3,2,1,0:T(4,128)} %bitcast.211) | data formatting | bytes 2097152
  17.9 35.8 %all_to_all.72 = f32[16,1,16384]{2,1,0:T(1,128)S(1)} all-to-all(f32[16,1,16384]{2,1,0:T(1,128)S(1)} %reshape.167), channel_id=1, replica_groups=mesh['pa'=16,'pb'=16] {'pb'}, dimensions={0} | all-to-all | bytes 2097152 | tf_op jit(solution)/shard_map/all_to_all | solution.py:97
  54.2 3.1 reduce.8
  57.3 8.0 %reshape.168 = f32[128,2,16,4,16]{4,3,2,1,0:T(4,128)} reshape(f32[16,16384]{1,0:T(8,128)S(1)} %reduce.8) | data formatting | bytes 2097152
  65.3 8.2 %copy.238 = f32[2,16,4,16,128]{3,4,2,1,0:T(8,128)S(1)} copy(f32[2,16,4,16,128]{3,2,1,0,4:T(4,128)} %bitcast.215) | data formatting | bytes 2097152 | tf_op jit(solution)/shard_map/all_to_all | solution.py:97
  73.6 5.2 copy.59
  78.8 6.1 %reshape.142 = f32[2,16,4,256,8,1]{3,4,0,2,1,5:T(8,128)S(1)} reshape(f32[2,16,4,16,16,8]{4,3,5,0,2,1:T(8,128)} %copy.59) | data formatting | bytes 2097152 | tf_op jit(solution)/shard_map/all_to_all | solution.py:97
  84.9 3.1 convolution_bitcast_fusion.1
  88.0 7.5 %copy.60 = f32[2,16,4,256,8]{1,4,2,0,3:T(8,128)} copy(f32[2,16,4,256,8]{3,4,0,2,1:T(8,128)S(1)} %convolution_bitcast_fusion.1) | data formatting | bytes 2097152 | tf_op jit(solution)/shard_map/qczxy,qpxk->pczky/transpose | solution.py:95
  95.5 7.3 %reshape.169 = f32[16,1,16384]{2,1,0:T(1,128)} reshape(f32[256,2,4,8,16]{4,3,2,1,0:T(8,128)} %bitcast.212) | data formatting | bytes 2097152
  102.8 10.2 %all-to-all-start.1 = ((f32[16,1,16384]{2,1,0:T(1,128)}), f32[16,1,16384]{2,1,0:T(1,128)S(1)}, u32[]{:S(2)}, u32[]{:S(2)}) async-start(f32[16,1,16384]{2,1,0:T(1,128)} %reshape.169), calls=%async_computation.1 | async-start | bytes 2097152 | tf_op jit(solution)/shard_map/all_to_all | solution.py:101
  113.0 1.1 fusion.271
  114.1 27.5 %all-to-all-done.1 = f32[16,1,16384]{2,1,0:T(1,128)S(1)} async-done(((f32[16,1,16384]{2,1,0:T(1,128)}), f32[16,1,16384]{2,1,0:T(1,128)S(1)}, u32[]{:S(2)}, u32[]{:S(2)}) %all-to-all-start.1) | async-done | bytes 1048608 | tf_op jit(solution)/shard_map/all_to_all | solution.py:101
  141.6 3.1 reduce.9
  144.7 4.8 reshape.170
  149.5 11.7 %copy.61 = f32[2,16,4,16,16,8]{4,5,2,3,1,0:T(8,128)} copy(f32[2,16,4,16,16,8]{1,5,2,0,4,3:T(8,128)} %bitcast.217) | data formatting | bytes 2097152 | tf_op jit(solution)/shard_map/all_to_all | solution.py:101
  161.2 17.1 %fusion.252 = f32[2,16,64,16,8]{2,3,0,4,1:T(8,128)S(1)} fusion(f32[2,2,64,64,1,1]{3,2,0,1,5,4:T(8,128)S(1)} %copy-done.4, f32[2,16,64,16,8,1]{3,4,2,1,0,5:T(8,128)} %bitcast.214), kind=kOutput, calls=%fused_computation.247 | convolution fusion | flops 402653184 | bytes 2162688 | tf_op jit(solution)/shard_map/qczxy,qpzk->pckxy/dot_general | solution.py:102
  178.9 1.8 fusion.249
  180.8 9.1 %copy.63 = f32[2,16,64,16,8]{3,0,4,1,2:T(2,128)} copy(f32[2,16,64,16,8]{2,3,0,4,1:T(8,128)S(1)} %fusion.249) | data formatting | bytes 2097152 | tf_op jit(solution)/shard_map/qckxy,qpzk->pczxy/transpose | solution.py:121
  189.9 13.0 %reshape.171 = f32[16,1,16384]{2,1,0:T(1,128)S(1)} reshape(f32[64,16,8,2,16]{4,3,2,1,0:T(2,128)} %bitcast.210) | data formatting | bytes 2097152
  202.9 32.1 %all_to_all.73 = f32[16,1,16384]{2,1,0:T(1,128)S(1)} all-to-all(f32[16,1,16384]{2,1,0:T(1,128)S(1)} %reshape.171), channel_id=1, replica_groups=mesh['pa'=16,'pb'=16] {'pa'}, dimensions={0} | all-to-all | bytes 2097152 | tf_op jit(solution)/shard_map/all_to_all | solution.py:124
  235.0 3.1 reduce.10
  238.2 13.3 %reshape.172 = f32[64,16,8,2,16]{4,3,2,1,0:T(2,128)} reshape(f32[16,16384]{1,0:T(8,128)S(1)} %reduce.10) | data formatting | bytes 2097152
  251.5 4.4 copy.64
  255.9 9.7 %copy.65 = f32[2,16,4,16,16,8]{4,3,5,0,2,1:T(8,128)} copy(f32[2,16,4,16,16,8]{4,5,2,3,1,0:T(8,128)S(1)} %bitcast.219) | data formatting | bytes 2097152 | tf_op jit(solution)/shard_map/all_to_all | solution.py:124
  265.6 6.1 %reshape.159 = f32[2,16,4,256,8,1]{3,4,0,2,1,5:T(8,128)S(1)} reshape(f32[2,16,4,16,16,8]{4,3,5,0,2,1:T(8,128)} %copy.65) | data formatting | bytes 2097152 | tf_op jit(solution)/shard_map/all_to_all | solution.py:124
  271.7 3.1 convolution_bitcast_fusion
  274.8 7.5 %copy.66 = f32[2,16,4,256,8]{1,4,2,0,3:T(8,128)} copy(f32[2,16,4,256,8]{3,4,0,2,1:T(8,128)S(1)} %convolution_bitcast_fusion) | data formatting | bytes 2097152 | tf_op jit(solution)/shard_map/qczky,qpxk->pczxy/transpose | solution.py:122
  282.4 7.1 %reshape.173 = f32[16,1,16384]{2,1,0:T(1,128)} reshape(f32[256,2,4,8,16]{4,3,2,1,0:T(8,128)} %bitcast.213) | data formatting | bytes 2097152
  289.5 6.0 %all-to-all-start.3 = ((f32[16,1,16384]{2,1,0:T(1,128)}), f32[16,1,16384]{2,1,0:T(1,128)}, u32[]{:S(2)}, u32[]{:S(2)}) async-start(f32[16,1,16384]{2,1,0:T(1,128)} %reshape.173), calls=%async_computation.3 | async-start | bytes 2097152 | tf_op jit(solution)/shard_map/all_to_all | solution.py:130
  295.5 1.5 fusion.262
  297.0 25.5 %all-to-all-done.3 = f32[16,1,16384]{2,1,0:T(1,128)} async-done(((f32[16,1,16384]{2,1,0:T(1,128)}), f32[16,1,16384]{2,1,0:T(1,128)}, u32[]{:S(2)}, u32[]{:S(2)}) %all-to-all-start.3) | async-done | bytes 1048608 | tf_op jit(solution)/shard_map/all_to_all | solution.py:130
  322.5 4.4 reduce.11
  326.9 4.8 reshape.174
  331.7 11.7 %copy.67 = f32[2,16,4,16,16,8]{4,5,3,2,1,0:T(8,128)} copy(f32[2,16,4,16,16,8]{1,5,2,0,4,3:T(8,128)} %bitcast.220) | data formatting | bytes 2097152 | tf_op jit(solution)/shard_map/all_to_all | solution.py:130
  343.4 15.5 %fusion.233 = f32[16,4,16,256,1]{3,2,0,1,4:T(8,128)S(1)} fusion(f32[2,256,128,1,1]{2,1,3,4,0:T(8,128)S(1)} %copy-done.3, f32[2,16,4,16,16,8]{4,5,3,2,1,0:T(8,128)} %copy.67), kind=kOutput, calls=%fused_computation.226 | convolution fusion | flops 805306368 | bytes 2359296 | tf_op jit(solution)/shard_map/qczxk,qyk->czxy/dot_general | solution.py:128
  359.7 74.3 %psum.14 = f32[16]{0:T(128)S(1)} all-reduce(f32[16]{0:T(128)S(1)} %fusion.270), channel_id=1, replica_groups=mesh['pa'=16,'pb'=16] {'pa','pb'}, use_global_device_ids=true, to_apply=%region_1.2 | all-reduce | flops 16 | bytes 128 | tf_op jit(solution)/shard_map/psum | solution.py:136
  434.0 0.8 multiply_reduce_fusion
  434.8 73.5 %psum.15 = f32[16]{0:T(128)S(1)} all-reduce(f32[16]{0:T(128)S(1)} %multiply_reduce_fusion), channel_id=1, replica_groups=mesh['pa'=16,'pb'=16] {'pa','pb'}, use_global_device_ids=true, to_apply=%region_3.4 | all-reduce | flops 16 | bytes 128 | tf_op jit(solution)/shard_map/psum | solution.py:139
  508.4 1.8 multiply_add_fusion
  510.2 40.5 %while.15 = (s32[]{:T(128)}, f32[16,4,16,256]{3,2,1,0:T(8,128)}, f32[16,4,16,256]{3,2,1,0:T(8,128)}, f32[16,16]{1,0:T(8,128)S(1)}, s32[16,4,16,256]{3,2,1,0:T(8,128)}, /*index=5*/f32[16,16,8]{1,0,2:T(8,128)S(1)}, s32[]{:T(128)}) while((s32[]{:T(128)}, f32[16,4,16,256]{3,2,1,0:T(8,128)}, f32[16,4,16,256]{3,2,1,0:T(8,128)}, ...), condition=%wide.region_5.6_spmd, body=%wide.region_4.5_spmd.sunk | while | flops 132907008 | bytes 10552917 | solution.py:150
  510.2 1.0 constant_dynamic-slice_fusion.4
  511.7 1.0 constant_dynamic-slice_fusion.5
  512.7 0.8 convolution_add_fusion.15
  513.5 0.8 convolution_add_fusion.16
  514.4 0.8 convolution_add_fusion.17
  515.2 0.8 convolution_add_fusion.18
  516.1 0.8 convolution_add_fusion.19
  519.5 0.9 copy_dynamic-update-slice_fusion.2
  520.3 1.0 constant_dynamic-slice_fusion.4
  521.9 1.0 constant_dynamic-slice_fusion.5
  522.8 0.8 convolution_add_fusion.15
  529.6 0.9 copy_dynamic-update-slice_fusion.2
  530.5 1.0 constant_dynamic-slice_fusion.4
  532.0 1.0 constant_dynamic-slice_fusion.5
  533.8 0.8 convolution_add_fusion.16
  539.7 0.9 copy_dynamic-update-slice_fusion.2
  540.6 1.0 constant_dynamic-slice_fusion.4
  542.1 1.0 constant_dynamic-slice_fusion.5
  543.1 0.8 convolution_add_fusion.15
  549.9 0.9 copy_dynamic-update-slice_fusion.2
  (58 shorter events, 24.3 us)
Async XLA Ops:
  0.0 1.2 copy-start
  88.0 25.0 %copy-start.2 = (f32[2,16,16,32,2,1]{3,5,4,2,1,0:T(1,128)S(1)}, f32[2,16,16,32,2,1]{3,5,4,2,1,0:T(1,128)}, u32[]{:S(2)}) copy-start(f32[2,16,16,32,2,1]{3,5,4,2,1,0:T(1,128)} %param.18) | copy-start | bytes 393220
  102.8 38.7 %all-to-all-start.1 = ((f32[16,1,16384]{2,1,0:T(1,128)}), f32[16,1,16384]{2,1,0:T(1,128)S(1)}, u32[]{:S(2)}, u32[]{:S(2)}) async-start(f32[16,1,16384]{2,1,0:T(1,128)} %reshape.169), calls=%async_computation.1 | async-start | bytes 2097152 | tf_op jit(solution)/shard_map/all_to_all | solution.py:101
  149.5 11.7 %copy-start.4 = (f32[2,2,64,64,1,1]{3,2,0,1,5,4:T(8,128)S(1)}, f32[2,2,64,64,1,1]{3,2,0,1,5,4:T(8,128)}, u32[]{:S(2)}) copy-start(f32[2,2,64,64,1,1]{3,2,0,1,5,4:T(8,128)} %constant.253) | copy-start | bytes 196612
  161.2 17.1 %copy-start.1 = (f32[1,16,16,32,2,1]{3,5,4,2,1,0:T(1,128)S(1)}, f32[1,16,16,32,2,1]{3,5,4,2,1,0:T(1,128)}, u32[]{:S(2)}) copy-start(f32[1,16,16,32,2,1]{3,5,4,2,1,0:T(1,128)} %get-tuple-element.205) | copy-start | bytes 196612
  161.2 17.8 %copy-start.10 = (f32[2,2,64,64,1,1]{3,2,0,1,5,4:T(8,128)S(1)}, f32[2,2,64,64,1,1]{3,2,0,1,5,4:T(8,128)}, u32[]{:S(2)}) copy-start(f32[2,2,64,64,1,1]{3,2,0,1,5,4:T(8,128)} %constant.254) | copy-start | bytes 196612
  274.8 20.6 %copy-start.6 = (f32[16,16]{1,0:T(8,128)S(1)}, f32[16,16]{1,0:T(8,128)}, u32[]{:S(2)}) copy-start(f32[16,16]{1,0:T(8,128)} %param.19) | copy-start | bytes 3076
  289.5 33.0 %all-to-all-start.3 = ((f32[16,1,16384]{2,1,0:T(1,128)}), f32[16,1,16384]{2,1,0:T(1,128)}, u32[]{:S(2)}, u32[]{:S(2)}) async-start(f32[16,1,16384]{2,1,0:T(1,128)} %reshape.173), calls=%async_computation.3 | async-start | bytes 2097152 | tf_op jit(solution)/shard_map/all_to_all | solution.py:130
  331.7 11.7 %copy-start.3 = (f32[2,256,128,1,1]{2,1,3,4,0:T(8,128)S(1)}, f32[2,256,128,1,1]{2,1,3,4,0:T(8,128)}, u32[]{:S(2)}) copy-start(f32[2,256,128,1,1]{2,1,3,4,0:T(8,128)} %constant.256) | copy-start | bytes 786436
  343.4 16.3 %copy-start.5 = (f32[16,16,8]{1,2,0:T(8,128)S(1)}, f32[16,16,8]{1,2,0:T(8,128)}, u32[]{:S(2)}) copy-start(f32[16,16,8]{1,2,0:T(8,128)} %param.23) | copy-start | bytes 24580
  343.4 165.0 %copy-start.9 = (f32[16]{0:T(128)S(1)}, f32[16]{0:T(128)}, u32[]{:S(2)}) copy-start(f32[16]{0:T(128)} %param.20) | copy-start | bytes 196
  343.4 165.0 %copy-start.7 = (f32[16]{0:T(128)S(1)}, f32[16]{0:T(128)}, u32[]{:S(2)}) copy-start(f32[16]{0:T(128)} %param.21) | copy-start | bytes 196
  343.4 166.8 %copy-start.8 = (f32[16,16]{1,0:T(8,128)S(1)}, f32[16,16]{1,0:T(8,128)}, u32[]{:S(2)}) copy-start(f32[16,16]{1,0:T(8,128)} %param.22) | copy-start | bytes 3076
where the time goes:
time: 559 us; the launch traced here: 551 us
  blocking collectives  216 us (39%)
  local copies, waits for them, and re-layouts  175 us (31%)
  matrix products  73 us (13%)
  waiting for transfers between devices  53 us (9%)
  other arithmetic  17.8 us (3%)
  starting transfers between devices  16.1 us (3%)
    psum x1, blocking collectives, on_device(): totals = lax.psum(jnp.sum(hidden, axis=(1, 2, 3)), ('pa', 'pb'))  74.3 us
    psum x1, blocking collectives, on_device(): lax.psum(jnp.sum(centered * centered, axis=(1, 2, 3)), ('pa', 'pb'))  73.5 us
    unnamed x31, local copies, waits for them, and re-layouts  68 us
    all_to_all x1, blocking collectives, on_device(): lax.all_to_all(spectrum, 'pb', split_axis=4, concat_axis=3, tiled=True)  35.8 us
    all_to_all x1, blocking collectives, on_device(): lax.all_to_all(backward, 'pa', split_axis=2, concat_axis=3, tiled=True)  32.1 us
    all_to_all x1, waiting for transfers between devices, on_device(): planes = lax.all_to_all(rows, 'pa', split_axis=3, concat_axis=2, tiled=True)  27.5 us
    dot_general x32, matrix products, kan_apply(): jnp.einsum('oi,i...->o...', spline_coef[:, :, basis], total, precision=HIGH)  26.8 us
    all_to_all x1, waiting for transfers between devices, on_device(): lax.all_to_all(rows_back, 'pb', split_axis=3, concat_axis=4, tiled=True)  25.5 us
  transfers between devices with their start and end apart: 2, of which 2 were waited for; matrix products, arithmetic and copies ran while one was open for 0% of the time, Pallas kernels for 0%

commit v1 on v0

v1 whole, which is shorter than its diff:
```python
import jax
import jax.numpy as jnp
import numpy as np
from jax import lax
from jax.experimental import pallas as pl
from jax.experimental.pallas import tpu as pltpu
from jax.sharding import PartitionSpec as P

NZ, NX, NY = 64, 256, 256
CELLS = NZ * NX * NY
BLOCK_CELLS = 4 * 16 * 256
EPSILON = 1e-05
EXACT = lax.Precision.HIGHEST
F32 = jnp.float32
B16 = jnp.bfloat16
BOTH = ("pa", "pb")
VMEM_LIMIT = 56 * 1024 * 1024

KX = np.array([[2 * p + k if p < 8 else 2 * p + k - 32 for k in range(2)] for p in range(16)])
KZ = np.array([j if j < 16 else j - 32 for j in range(32)])
KY = np.arange(16)


def split_table(table):
    high = jnp.asarray(table, F32).astype(B16)
    high = np.asarray(table, np.float32).astype(jnp.bfloat16)
    low = (np.asarray(table, np.float64) - high.astype(np.float64)).astype(jnp.bfloat16)
    return high, low


def rotation(angle, sign):
    cosine, sine = np.cos(angle), np.sin(angle)
    return np.stack([np.stack([cosine, -sign * sine]), np.stack([sign * sine, cosine])])


def tables():
    same_ky = np.eye(16)
    same_x = np.eye(4)
    angle = 2 * np.pi * (np.arange(NY)[:, None] * KY % NY) / NY
    y_part = np.stack([np.cos(angle), -np.sin(angle)], axis=1)
    y_forward = np.einsum("jJ,ypk->jyJpk", same_x, y_part).reshape(4, NY, 128)
    weight = np.where(KY == 0, 1.0, 2.0) / CELLS
    y_back = np.einsum("jJ,ypk,k->jJpky", same_x, y_part, weight).reshape(4, 128, NY)
    angle = 2 * np.pi * (KX[:, :, None] * np.arange(16) % NX) / NX
    turn = rotation(angle, -1.0)
    x_forward = np.einsum("qpahx,kK->qhakxpK", turn, same_ky).reshape(1024, 512)
    turn = rotation(angle, 1.0)
    x_back = np.einsum("qpahx,kK->phakxqK", turn, same_ky).reshape(2, 512, 512)
    z = 4 * np.arange(16)[None, :] + np.arange(4)[:, None]
    parts = []
    for frequencies in (KZ, -KZ):
        angle = 2 * np.pi * (z[:, :, None] * frequencies % NZ) / NZ
        parts.append(np.einsum("qpzaj,hH->pzhaqHj", rotation(angle, -1.0), np.eye(2)).reshape(256, 128))
    z_forward = np.concatenate(parts, axis=1)
    angle = 2 * np.pi * (z[:, :, None] * KZ % NZ) / NZ
    z_back = np.einsum("qpzaj->qzapj", rotation(angle, 1.0)).reshape(128, 64)
    return y_forward, y_back, x_forward, x_back, z_forward, z_back


Y_FORWARD, Y_BACK, X_FORWARD, X_BACK, Z_FORWARD, Z_BACK = tables()
PHASE = np.stack([np.cos(2 * np.pi * np.arange(16) / 16), np.sin(2 * np.pi * np.arange(16) / 16)]).astype(np.float32)


def split(values):
    high = values.astype(B16)
    return high, (values - high.astype(F32)).astype(B16)


def dot(left, right):
    return jnp.dot(left, right, preferred_element_type=F32)


def dot_nt(left, right, precision=None):
    return lax.dot_general(left, right, (((1,), (1,)), ((), ())), precision=precision, preferred_element_type=F32)


def dot_exact(left, right):
    return jnp.dot(left, right, precision=EXACT, preferred_element_type=F32)


def iota(shape, axis):
    return lax.broadcasted_iota(jnp.int32, shape, axis)


def phase_index(kxp, kxl, block):
    return (((2 * kxp + kxl) % 16) * block) % 16


def forward_kernel(
    ids_ref, phase_ref, left_ref, right_ref, weight_ref, y_ref, x_high_ref, x_low_ref, out_ref, sent_ref, half_ref, rows_ref
):
    pa, pb = ids_ref[0], ids_ref[1]
    rows_ref[:, 0:32] = weight_ref[...]
    wanted = jnp.where(pa < 8, 1, 0)
    chosen = rows_ref[pl.ds(wanted, 512, stride=2), :]
    sent_ref[...] = jnp.concatenate([chosen[128 * q : 128 * (q + 1), 0:32] for q in range(4)], axis=1)
    total = jnp.zeros((256, 128), F32)
    for xj in range(4):
        piece = jnp.concatenate(
            [left_ref[pl.ds(xj, 256, stride=4), :], right_ref[pl.ds(xj, 256, stride=4), :]], axis=1
        )
        high, low = split(piece)
        product = dot(high, y_ref[xj])
        total = total + product[:, 0:128] + product[:, 128:256] + dot(low, y_ref[xj, :, 0:128])
    half_ref[...] = total
    lines = jnp.concatenate(
        [
            jnp.concatenate([half_ref[pl.ds(z * 4 + x4, 16, stride=16), :] for z in range(4)], axis=0)
            for x4 in range(4)
        ],
        axis=1,
    )
    high, low = split(lines)
    first = dot_nt(x_high_ref[...], jnp.concatenate([high, low], axis=0))
    rows = first[:, 0:64] + first[:, 64:128] + dot_nt(x_low_ref[...], high)
    rows = jnp.concatenate([rows[0:512], rows[512:1024]], axis=1)
    turned = pltpu.roll(rows, 64, axis=1)
    sign = jnp.where(iota((16, 128), 1) < 64, 1.0, -1.0).astype(F32)
    for kxl in range(2):
        for kxp in range(16):
            index = phase_index(kxp, kxl, pb)
            start = (kxl * 16 + kxp) * 16
            value = (
                rows[start : start + 16] * phase_ref[0, index]
                + turned[start : start + 16] * (sign * phase_ref[1, index])
            )
            out_ref[pl.ds(kxp * 32 + kxl, 16, stride=2), :] = value


def local_kernel(
    left_ref, right_ref, index_ref, index2_ref, map_ref, base_ref, coef_ref,
    hidden_ref, level_ref, stat_ref, kan_ref, shift_ref,
):
    high, low = split(map_ref[...])
    zero = jnp.zeros((16, 16), B16)
    maps = jnp.concatenate(
        [jnp.concatenate([high, high], axis=1), jnp.concatenate([low, zero], axis=1)], axis=0
    )

    def step(x, total):
        sides = []
        for z in range(4):
            rows = pl.ds(z * 16 + x, 16, stride=64)
            high, low = split(jnp.concatenate([left_ref[rows, :], right_ref[rows, :]], axis=1))
            both = dot(maps, jnp.concatenate([high, low], axis=0))
            value = both[0:16] + both[16:32]
            total = total + value
            start = pl.multiple_of(x * 64 + z * 16, 16)
            hidden_ref[pl.ds(start, 16), :] = value
            level_ref[pl.ds(start, 16), :] = jnp.concatenate(
                [index_ref[rows, :], index2_ref[rows, :]], axis=1
            ).astype(F32)
        return total

    total = lax.fori_loop(0, 16, step, jnp.zeros((16, 256), F32))
    mean = jnp.sum(total, axis=1, keepdims=True) * (1.0 / BLOCK_CELLS)

    def spread(part, total):
        for z in range(4):
            start = pl.multiple_of(part * 64 + z * 16, 16)
            away = hidden_ref[pl.ds(start, 16), :] - mean
            total = total + away * away
        return total

    total = lax.fori_loop(0, 16, spread, jnp.zeros((16, 256), F32))
    squares = jnp.sum(total, axis=1, keepdims=True)
    first = iota((16, 128), 1) == 0
    stat_ref[0:16, :] = jnp.where(first, mean, 0.0)
    stat_ref[16:32, :] = jnp.where(first, squares, 0.0)
    last = coef_ref[:, 7, :]
    pieces = [coef_ref[:, basis, :] - last for basis in range(7)] + [base_ref[...]]
    high, low = split(jnp.concatenate(pieces, axis=1))
    kan_ref[0:16, 0:128] = high
    kan_ref[0:16, 128:256] = high
    kan_ref[16:32, 0:128] = low
    kan_ref[16:32, 128:256] = jnp.zeros((16, 128), B16)
    shift_ref[...] = jnp.broadcast_to(jnp.sum(last, axis=1, keepdims=True), (16, 128))


def mix_kernel(
    ids_ref, phase_ref, got_ref, weight_ref, partner_ref, map_ref, stat_ref, z_ref, back_ref, out_ref, rows_ref
):
    pa, pb = ids_ref[0], ids_ref[1]
    total = jnp.sum(got_ref[...].reshape(16, 4, 8, 128), axis=1)
    total = total + pltpu.roll(total, 4, axis=1)
    total = total + pltpu.roll(total, 2, axis=1)
    rows_ref[...] = total.reshape(128, 128)
    lines = jnp.concatenate([rows_ref[pl.ds(0, 16, stride=8), :], rows_ref[pl.ds(1, 16, stride=8), :]], axis=0)
    lines = lines.T
    lines = jnp.concatenate([lines[16 * q : 16 * (q + 1)] for q in range(8)], axis=1)
    modes = dot_exact(lines, z_ref[...])
    real = [modes[:, 32 * k : 32 * k + 32] for k in range(2)]
    imag = [modes[:, 64 + 32 * k : 96 + 32 * k] for k in range(2)]
    lower = pa < 8
    far_real = jnp.where(lower, modes[:, 128:160], modes[:, 160:192])
    far_imag = jnp.where(lower, modes[:, 192:224], modes[:, 224:256])
    odd = iota((32, 32), 0) % 2 == 1
    twice = (iota((32, 16), 0) // 2 == iota((32, 16), 1)).astype(F32)
    map_rows = dot_exact(twice, map_ref[...])
    mixed_real = jnp.zeros((32, 32), F32)
    mixed_imag = jnp.zeros((32, 32), F32)
    local_real = jnp.zeros((32, 32), F32)
    local_imag = jnp.zeros((32, 32), F32)
    partner_real = jnp.zeros((16, 32), F32)
    partner_imag = jnp.zeros((16, 32), F32)
    for i in range(16):
        mode_real = jnp.where(odd, real[1][i : i + 1], real[0][i : i + 1])
        mode_imag = jnp.where(odd, imag[1][i : i + 1], imag[0][i : i + 1])
        weight_real = weight_ref[32 * i : 32 * i + 32, :]
        weight_imag = weight_ref[512 + 32 * i : 544 + 32 * i, :]
        mixed_real = mixed_real + weight_real * mode_real - weight_imag * mode_imag
        mixed_imag = mixed_imag + weight_real * mode_imag + weight_imag * mode_real
        column = map_rows[:, i : i + 1]
        local_real = local_real + column * mode_real
        local_imag = local_imag + column * mode_imag
        row = 16 * (i % 8)
        lane = 32 * (i // 8)
        weight_real = partner_ref[row : row + 16, lane : lane + 32]
        weight_imag = partner_ref[row : row + 16, 64 + lane : 96 + lane]
        mode_real = far_real[i : i + 1]
        mode_imag = far_imag[i : i + 1]
        partner_real = partner_real + weight_real * mode_real + weight_imag * mode_imag
        partner_imag = partner_imag + weight_imag * mode_real - weight_real * mode_imag
    origin = jnp.logical_and(
        jnp.logical_and(pa == 0, pb == 0), jnp.logical_and(iota((32, 32), 0) % 2 == 0, iota((32, 32), 1) == 0)
    )
    centre = jnp.where(origin, mixed_real, 0.0)
    moved_real = jnp.where(origin, 0.0, mixed_real)
    moved_imag = jnp.where(origin, 0.0, mixed_imag)
    own = jnp.where(pb == 0, 0.5, 2.0)
    cross = jnp.where(pb == 0, 2.0, 4.0)
    power = own * (moved_real * moved_real + moved_imag * moved_imag)
    power = power + cross * (moved_real * local_real + moved_imag * local_imag)
    chosen = jnp.where(lower, 0, 1)
    pick = (iota((16, 32), 1) == 2 * iota((16, 32), 0) + chosen).astype(F32)
    picked = dot_exact(pick, jnp.concatenate([moved_real, moved_imag], axis=1))
    source, target = iota((32, 32), 0), iota((32, 32), 1)
    turned = jnp.logical_and(target != 16, source == (32 - target) % 32).astype(F32)
    near = dot_exact(jnp.concatenate([picked[:, 0:32], picked[:, 32:64]], axis=0), turned)
    partner_real = jnp.where(pa == 0, picked[:, 0:32], partner_real)
    partner_imag = jnp.where(pa == 0, picked[:, 32:64], partner_imag)
    pair = jnp.where(pb == 0, jnp.where(pa == 0, 0.5, 1.0), 0.0) * (
        near[0:16] * partner_real - near[16:32] * partner_imag
    )
    sums = jnp.concatenate(
        [
            power * (1.0 / CELLS),
            pair * (1.0 / CELLS),
            stat_ref[:, 0:32],
            centre * (1.0 / CELLS),
            jnp.zeros((16, 32), F32),
        ],
        axis=0,
    )
    sums = dot_nt(jnp.ones((8, 32), F32), sums, EXACT)
    out_ref[pl.ds(2, 256, stride=3), :] = jnp.broadcast_to(sums[0:1], (256, 128))
    order = (iota((32, 32), 1) == 2 * (iota((32, 32), 0) % 16) + iota((32, 32), 0) // 16).astype(F32)
    mixed = dot_exact(order, jnp.concatenate([mixed_real, mixed_imag], axis=1))
    planes = dot_nt(back_ref[...], mixed, EXACT)
    sign = jnp.where(iota((16, 128), 1) < 64, -1.0, 1.0).astype(F32)
    for kxl in range(2):
        value = jnp.concatenate(
            [planes[16 * q : 16 * (q + 1), 16 * kxl : 16 * kxl + 16] for q in range(8)], axis=1
        )
        other = pltpu.roll(value, 64, axis=1) * sign
        for block in range(16):
            index = phase_index(pa, kxl, block)
            out_ref[pl.ds(block * 3 + kxl, 16, stride=48), :] = (
                value * phase_ref[0, index] + other * phase_ref[1, index]
            )


def column(row):
    eye = (iota((16, 16), 0) == iota((16, 16), 1)).astype(F32)
    return dot_nt(eye, jnp.broadcast_to(row, (8, 16)), EXACT)[:, 0:1]


def output_kernel(
    got_ref, hidden_ref, level_ref, kan_ref, constant_ref, gain_ref, bias_ref,
    x_high_ref, x_low_ref, y_high_ref, y_low_ref, out_ref, spec_ref, result_ref, sems,
):
    stats = got_ref[pl.ds(2, 256, stride=3), :]
    sums = jnp.sum(stats, axis=0, keepdims=True)
    mean = sums * (1.0 / 256)
    away = stats - mean
    between = jnp.sum(away * away, axis=0, keepdims=True) * float(BLOCK_CELLS)
    lane = iota((1, 128), 1)
    is_mean = jnp.logical_and(lane >= 48, lane < 64)
    is_centre = jnp.logical_and(lane >= 80, lane < 112)
    variance = jnp.where(is_mean, between, jnp.where(lane < 80, sums, 0.0)) * (1.0 / CELLS)
    mean = jnp.where(is_mean, mean, jnp.where(is_centre, sums, 0.0))
    lane, row = iota((16, 128), 1), iota((16, 128), 0)
    owner = jnp.where(
        lane < 32, lane // 2, jnp.where(lane < 80, lane % 16, jnp.where(lane < 112, (lane - 80) // 2, -1))
    )
    pick = (owner == row).astype(F32)
    mean = dot_nt(pick, jnp.broadcast_to(mean, (8, 128)), EXACT)[:, 0:1]
    variance = dot_nt(pick, jnp.broadcast_to(variance, (8, 128)), EXACT)[:, 0:1]
    scale = column(gain_ref[...]) * lax.rsqrt(variance + EPSILON)
    mean = jnp.broadcast_to(jnp.concatenate([mean] * 4, axis=0), (64, 128))
    scale = jnp.broadcast_to(jnp.concatenate([scale] * 4, axis=0), (64, 128))
    bias = jnp.broadcast_to(jnp.concatenate([column(bias_ref[...])] * 4, axis=0), (64, 128))
    lines = jnp.concatenate(
        [
            got_ref[pl.ds(kxl + 384 * half, 128, stride=3), :].T
            for kxl in range(2)
            for half in range(2)
        ],
        axis=1,
    )
    high, low = split(lines)
    total = jnp.zeros((64, 512), F32)
    for part in range(2):
        rows = slice(64 * part, 64 * part + 64)
        both = dot(jnp.concatenate([high[rows], low[rows]], axis=0), x_high_ref[part])
        total = total + both[0:64] + both[64:128] + dot(high[rows], x_low_ref[part])
    lines = jnp.concatenate([total[:, 128 * x4 : 128 * (x4 + 1)] for x4 in range(4)], axis=0)
    high, low = split(lines)
    both = jnp.concatenate([high, low], axis=0)
    for xj in range(4):
        product = dot(both, y_high_ref[xj])
        value = product[0:256] + product[256:512] + dot(high, y_low_ref[xj])
        for x4 in range(4):
            start = (4 * x4 + xj) * 64
            spec_ref[start : start + 64, :] = value[64 * x4 : 64 * x4 + 64]
    weights = kan_ref[...]
    constant = constant_ref[...]
    copies = []
    for half in range(2):
        lanes = slice(128 * half, 128 * half + 128)

        def step(x, carry, half=half, lanes=lanes):
            rows = pl.ds(pl.multiple_of(x * 64, 64), 64)
            hidden = spec_ref[rows, lanes] + hidden_ref[rows, lanes]
            normed = (hidden - mean) * scale + bias
            level = level_ref[rows, lanes]
            local = jnp.clip(normed * 1.25 + (2.5 - level), 0.0, 1.0)
            other = 1.0 - local
            square = local * local
            cube = square * local
            p0 = other * other * other * (1.0 / 6.0)
            p3 = cube * (1.0 / 6.0)
            p1 = 0.5 * cube - square + 2.0 / 3.0
            p2 = 0.5 * (square + local - cube) + 1.0 / 6.0
            at = [level == float(k) for k in range(5)]
            zero = jnp.zeros_like(p0)
            pieces = [p0, p1, p2, p3]
            features = []
            for basis in range(7):
                value = zero
                for r in range(4):
                    if 0 <= basis - r <= 4:
                        value = jnp.where(at[basis - r], pieces[r], value)
                features.append(value)
            features.append(0.5 * normed * (1.0 + jnp.tanh(0.5 * normed)))
            parts = [split(value) for value in features]
            columns = []
            for z in range(4):
                columns.append(
                    jnp.concatenate(
                        [part[0][16 * z : 16 * z + 16] for part in parts]
                        + [part[1][16 * z : 16 * z + 16] for part in parts],
                        axis=0,
                    )
                )
            product = dot(weights, jnp.concatenate(columns, axis=1))
            for z in range(4):
                value = product[0:16, 128 * z : 128 * z + 128] + product[16:32, 128 * z : 128 * z + 128]
                result_ref[half, pl.ds(z * 16 + x, 16, stride=64), :] = value + constant
            return carry

        lax.fori_loop(0, 16, step, 0)
        copy = pltpu.make_async_copy(result_ref.at[half], out_ref.at[:, lanes], sems.at[half])
        copy.start()
        copies.append(copy)
    for copy in copies:
        copy.wait()


def whole():
    return pl.BlockSpec(memory_space=pltpu.VMEM)


def scalars():
    return pl.BlockSpec(memory_space=pltpu.SMEM)


def sides(rows):
    return [pl.BlockSpec((rows, 128), lambda step, h=h: (0, h)) for h in range(2)]


def params():
    return pltpu.CompilerParams(vmem_limit_bytes=VMEM_LIMIT)


def cost(flops, moved):
    return pl.CostEstimate(flops=flops, bytes_accessed=moved, transcendentals=0)


def shape(dims, dtype=F32):
    return jax.ShapeDtypeStruct(dims, dtype)


def on_device(
    field, spline_index, spec_weight, local_weight, bn_gain, bn_shift, base_weight, spline_coef
):
    ids = jnp.stack([lax.axis_index("pa"), lax.axis_index("pb")]).astype(jnp.int32)
    phase = jnp.asarray(PHASE)
    field = field.reshape(1024, 256)
    index = spline_index.reshape(1024, 256)
    weight = jnp.transpose(spec_weight, (0, 1, 2, 4, 5, 3)).reshape(1024, 32)
    y_high, y_low = split_table(Y_FORWARD)
    x_high, x_low = split_table(X_FORWARD)
    sent, own = pl.pallas_call(
        forward_kernel,
        grid=(1,),
        out_shape=(shape((512, 128)), shape((128, 128))),
        in_specs=[scalars(), scalars(), *sides(1024)] + [whole()] * 4,
        out_specs=(whole(), whole()),
        scratch_shapes=[pltpu.VMEM((256, 128), F32), pltpu.VMEM((1024, 128), F32)],
        compiler_params=params(),
        cost_estimate=cost(4 * 10**8, 4 * 10**6),
        name="forward",
    )(
        ids, phase, field, field, weight,
        jnp.asarray(np.concatenate([y_high, y_low], axis=2)), jnp.asarray(x_high), jnp.asarray(x_low),
    )
    path = [0]
    while path[-1] != 8:
        path.append(15 - path[-1] if path[-1] < 8 else 16 - path[-1])
    partner = lax.ppermute(own, BOTH, [(16 * a, 16 * b) for a, b in zip(path[:-1], path[1:])])
    got = lax.all_to_all(sent.reshape(256, 2, 128), BOTH, 0, 0, tiled=True).reshape(512, 128)
    hidden, level, stat, kan, constant = pl.pallas_call(
        local_kernel,
        grid=(1,),
        out_shape=(
            shape((1024, 256)), shape((1024, 256)), shape((32, 128)), shape((32, 256), B16), shape((16, 128)),
        ),
        in_specs=sides(1024) + sides(1024) + [whole()] * 3,
        out_specs=(whole(),) * 5,
        compiler_params=params(),
        cost_estimate=cost(10**8, 4 * 10**6),
        name="local",
    )(field, field, index, index, local_weight, base_weight, jnp.transpose(spline_coef, (0, 2, 1)))
    back = pl.pallas_call(
        mix_kernel,
        out_shape=shape((768, 128)),
        in_specs=[scalars(), scalars()] + [whole()] * 7,
        out_specs=whole(),
        scratch_shapes=[pltpu.VMEM((128, 128), F32)],
        compiler_params=params(),
        cost_estimate=cost(10**7, 10**6),
        name="mix",
    )(
        ids, phase, got, weight, partner, local_weight, stat,
        jnp.asarray(Z_FORWARD, F32), jnp.asarray(Z_BACK, F32),
    )
    back = lax.all_to_all(back.reshape(256, 3, 128), BOTH, 0, 0, tiled=True).reshape(768, 128)
    x_high, x_low = split_table(X_BACK)
    y_high, y_low = split_table(Y_BACK)
    output = pl.pallas_call(
        output_kernel,
        out_shape=shape((1024, 256)),
        in_specs=[whole()] * 11,
        out_specs=pl.BlockSpec(memory_space=pl.ANY),
        scratch_shapes=[
            pltpu.VMEM((1024, 256), F32),
            pltpu.VMEM((2, 1024, 128), F32),
            pltpu.SemaphoreType.DMA((2,)),
        ],
        compiler_params=params(),
        cost_estimate=cost(10**9, 6 * 10**6),
        name="output",
    )(
        back, hidden, level, kan, constant, bn_gain.reshape(1, 16), bn_shift.reshape(1, 16),
        jnp.asarray(x_high), jnp.asarray(x_low), jnp.asarray(y_high), jnp.asarray(y_low),
    )
    return output.reshape(16, 4, 16, 256)


def solution(mesh):
    in_specs = (
        P(None, "pa", "pb", None),
        P(None, "pa", "pb", None),
        P(None, None, None, None, "pa", "pb"),
        P(),
        P(),
        P(),
        P(),
        P(),
    )
    out_specs = P(None, "pa", "pb", None)
    return jax.shard_map(
        on_device, mesh=mesh, in_specs=in_specs, out_specs=out_specs, check_vma=False
    )
```

time: 559 us -> 83.8 us (0.15); the launches traced: 551 us -> 83.5 us
  blocking collectives: 216 us -> 27 us
  local copies, waits for them, and re-layouts: 175 us -> 2.78 us
  matrix products: 73 us -> 0 us
  waiting for transfers between devices: 53 us -> 0.01 us
  Pallas kernels: 0 us -> 26.8 us
  other arithmetic: 17.8 us -> 0.59 us
  starting transfers between devices: 16.1 us -> 26.3 us
    psum x2 -> x0, blocking collectives: 148 us -> none  [the longest x1 74.3 us: on_device(): totals = lax.psum(jnp.sum(hidden, axis=(1, 2, 3)), ('pa', 'pb'))]
    dot_general x43 -> x0, matrix products: 73 us -> none  [the longest x32 26.8 us: kan_apply(): jnp.einsum('oi,i...->o...', spline_coef[:, :, basis], total, precision=HIGH)]
    unnamed x31 -> x6, local copies, waits for them, and re-layouts: 68 us -> 0.7 us
    all_to_all x9 -> x0, local copies, waits for them, and re-layouts: 63.6 us -> none  [the longest x3 20.2 us: on_device(): lax.all_to_all(backward, 'pa', split_axis=2, concat_axis=3, tiled=True)]
    all_to_all x2 -> x1, waiting for transfers between devices: 53 us -> 0.01 us  [on_device(): lax.all_to_all(sent.reshape(256, 2, 128), BOTH, 0, 0, tiled=True)]
    all_to_all x2 -> x1, blocking collectives: 67.9 us -> 27 us  [on_device(): lax.all_to_all(back.reshape(256, 3, 128), BOTH, 0, 0, tiled=True)]
    transpose x4 -> x0, local copies, waits for them, and re-layouts: 30.5 us -> none  [the longest x1 9.09 us: on_device(): backward = jnp.einsum('qckxy,qpzk->pczxy', mixed, z_inverse, precision=HIGH)]
    pallas_call x0 -> x4, Pallas kernels: none -> 26.8 us  [the longest x1 12.5 us: on_device(): pl.pallas_call(output_kernel, out_shape=shape((1024, 256)), in_specs=[who...]
  transfers between devices with their start and end apart: 2 -> 2, of which waited for: 2 -> 0; matrix products, arithmetic and copies ran while one was open for 0% -> 0% of each run, Pallas kernels for 0% -> 7%
where the time goes in v1:
time: 83.8 us; the launch traced here: 83.5 us
  blocking collectives  27 us (32%)
  Pallas kernels  26.8 us (32%)
  starting transfers between devices  26.3 us (31%)
  local copies, waits for them, and re-layouts  2.78 us (3%)
    all_to_all x1, blocking collectives, on_device(): lax.all_to_all(back.reshape(256, 3, 128), BOTH, 0, 0, tiled=True)  27 us
    all_to_all x1, starting transfers between devices, on_device(): lax.all_to_all(sent.reshape(256, 2, 128), BOTH, 0, 0, tiled=True)  15.7 us
    pallas_call x1, Pallas kernels, on_device(): pl.pallas_call(output_kernel, out_shape=shape((1024, 256)), in_specs=[who...  12.5 us
    ppermute x1, starting transfers between devices, on_device(): lax.ppermute(own, BOTH, [(16 * a, 16 * b) for a, b in zip(path[:-1], path...  10.7 us
    pallas_call x1, Pallas kernels, on_device(): pl.pallas_call(local_kernel, grid=(1,), out_shape=(shape((1024, 256)), sh...  6.05 us
    pallas_call x1, Pallas kernels, on_device(): pl.pallas_call(forward_kernel, grid=(1,), out_shape=(shape((512, 128)), s...  4.29 us
    pallas_call x1, Pallas kernels, on_device(): pl.pallas_call(mix_kernel, out_shape=shape((768, 128)), in_specs=[scalars...  3.94 us
  transfers between devices with their start and end apart: 2, of which 0 were waited for; matrix products, arithmetic and copies ran while one was open for 0% of the time, Pallas kernels for 7%

profile of v1, /device:TPU:1, one launch (start us, length us, event | category | flops | bytes accessed | tf_op | source)
XLA Modules:
  0.0 83.5 jit_solution(13349803237666356819)
XLA Ops:
  0.0 0.6 pad_add_fusion.ids_ref
  0.6 4.3 %forward.1 = (f32[512,128]{1,0:T(8,128)}, f32[128,128]{1,0:T(8,128)}) custom-call(s32[2]{0:T(128)} %pad_add_fusion.ids_ref, f32[2,16]{1,0:T(2,128)} %constant.27.clone.phase_ref, f32[1024,256]{1,0:T(8,128)} %bitcast.13, f32[1024,256]{1,0:T(8,128)} %bitcast.14, f32[1024,32]{1,0:T(8,128)} %bitcast.19, bf16[4,256,256]{2,1,0:T(8,128)(2,1)} %constant.28.clone.y_ref, ...), custom_call_target="tpu_custom_call" | custom-call | flops 400000000 | bytes 4000000 | tf_op jit(solution)/shard_map/forward/pallas_call | solution.py:414
  4.9 0.0 copy-start.2
  4.9 15.7 %all-to-all-start = ((f32[256,2,128]{2,1,0:T(2,128)}), f32[256,2,128]{2,1,0:T(2,128)S(1)}, u32[]{:S(2)}, u32[]{:S(2)}) async-start(f32[256,2,128]{2,1,0:T(2,128)} %bitcast.22), calls=%async_computation | async-start | bytes 524288 | tf_op jit(solution)/shard_map/all_to_all | solution.py:432
  20.6 0.0 copy-done.2
  20.6 10.7 %collective-permute-start = (f32[128,128]{1,0:T(8,128)S(1)}, f32[128,128]{1,0:T(8,128)S(1)}, u32[]{:S(2)}, u32[]{:S(2)}) collective-permute-start(f32[128,128]{1,0:T(8,128)S(1)} %copy-done.2), channel_id=1, source_target_pairs={{0,240},{240,16},{16,224},{224,32},{32,208},{208,48},{48,192},{192... | collective-permute-start | bytes 196616 | tf_op jit(solution)/shard_map/ppermute | solution.py:431
  31.3 6.0 %local.1 = (f32[1024,256]{1,0:T(8,128)}, f32[1024,256]{1,0:T(8,128)}, f32[32,128]{1,0:T(8,128)}, bf16[32,256]{1,0:T(8,128)(2,1)}, f32[16,128]{1,0:T(8,128)}) custom-call(f32[1024,256]{1,0:T(8,128)} %bitcast.15, f32[1024,256]{1,0:T(8,128)} %bitcast.16, s32[1024,256]{1,0:T(8,128)} %bitcast.17, s32[1024,256]{1,0:T(8,128)} %bitcast.18, f32[16,16]{1,0:T(8,128)} %map_ref.3, ...), custom_call_target="tpu_custom_call" | custom-call | flops 100000000 | bytes 4000000 | tf_op jit(solution)/shard_map/local/pallas_call | solution.py:433
  37.3 0.0 collective-permute-done.partner_ref
  37.3 0.0 copy-start.1
  37.3 0.0 all-to-all-done
  37.3 0.0 copy-start
  37.3 0.6 copy-done.1
  37.9 0.1 copy-done
  38.0 3.9 %mix.1 = f32[768,128]{1,0:T(8,128)} custom-call(s32[2]{0:T(128)} %pad_add_fusion.ids_ref, f32[2,16]{1,0:T(2,128)} %constant.27.clone.phase_ref, f32[512,128]{1,0:T(8,128)} %bitcast.21, f32[1024,32]{1,0:T(8,128)} %bitcast.20, f32[128,128]{1,0:T(8,128)} %copy-done.1, f32[16,16]{1,0:T(8,128)} %map_ref.3, f32[32,128]{1,0:T(8,128)} %get-tuple-element.14.stat_ref, ...), custom_call_target="tpu_custom_call" | custom-call | flops 10000000 | bytes 1000000 | tf_op jit(solution)/shard_map/mix/pallas_call | solution.py:445
  42.0 1.2 %reshape.35 = f32[256,3,128]{2,1,0:T(4,128)S(1)} reshape(f32[768,128]{1,0:T(8,128)} %mix.1) | data formatting | bytes 786432 | tf_op jit(solution)/shard_map/reshape | solution.py:458
  43.1 27.0 %all_to_all.10 = f32[256,3,128]{2,1,0:T(4,128)S(1)} all-to-all(f32[256,3,128]{2,1,0:T(4,128)S(1)} %reshape.35), channel_id=1, replica_groups=mesh['pa'=16,'pb'=16] {'pa','pb'}, dimensions={0} | all-to-all | bytes 786432 | tf_op jit(solution)/shard_map/all_to_all | solution.py:458
  70.1 0.9 %reshape.36.got_ref = f32[768,128]{1,0:T(8,128)} reshape(f32[256,3,128]{2,1,0:T(4,128)S(1)} %all_to_all.10) | data formatting | bytes 786432 | tf_op jit(solution)/shard_map/reshape | solution.py:458
  71.0 12.5 %output.1 = f32[1024,256]{1,0:T(8,128)} custom-call(f32[768,128]{1,0:T(8,128)} %reshape.36.got_ref, f32[1024,256]{1,0:T(8,128)} %get-tuple-element.15.hidden_ref, f32[1024,256]{1,0:T(8,128)} %get-tuple-element.16.level_ref, bf16[32,256]{1,0:T(8,128)(2,1)} %get-tuple-element.17.kan_ref, f32[16,128]{1,0:T(8,128)} %get-tuple-element.18.constant_ref, ...), custom_call_target="tpu_custom_call" | custom-call | flops 1000000000 | bytes 6000000 | tf_op jit(solution)/shard_map/output/pallas_call | solution.py:461
Async XLA Ops:
  4.9 15.7 %copy-start.2 = (f32[128,128]{1,0:T(8,128)S(1)}, f32[128,128]{1,0:T(8,128)}, u32[]{:S(2)}) copy-start(f32[128,128]{1,0:T(8,128)} %get-tuple-element.13) | copy-start | bytes 196612
  4.9 32.4 %all-to-all-start = ((f32[256,2,128]{2,1,0:T(2,128)}), f32[256,2,128]{2,1,0:T(2,128)S(1)}, u32[]{:S(2)}, u32[]{:S(2)}) async-start(f32[256,2,128]{2,1,0:T(2,128)} %bitcast.22), calls=%async_computation | async-start | bytes 524288 | tf_op jit(solution)/shard_map/all_to_all | solution.py:432
  20.6 16.7 %collective-permute-start = (f32[128,128]{1,0:T(8,128)S(1)}, f32[128,128]{1,0:T(8,128)S(1)}, u32[]{:S(2)}, u32[]{:S(2)}) collective-permute-start(f32[128,128]{1,0:T(8,128)S(1)} %copy-done.2), channel_id=1, source_target_pairs={{0,240},{240,16},{16,224},{224,32},{32,208},{208,48},{48,192},{192... | collective-permute-start | bytes 196616 | tf_op jit(solution)/shard_map/ppermute | solution.py:431
  37.3 0.6 copy-start.1
  37.3 0.7 copy-start

commit v2 on v1

v2 whole, which is shorter than its diff:
```python
import jax
import jax.numpy as jnp
import numpy as np
from jax import lax
from jax.experimental import pallas as pl
from jax.experimental.pallas import tpu as pltpu
from jax.sharding import PartitionSpec as P

NZ, NX, NY = 64, 256, 256
CELLS = NZ * NX * NY
BLOCK_CELLS = 4 * 16 * 256
EPSILON = 1e-05
EXACT = lax.Precision.HIGHEST
F32 = jnp.float32
B16 = jnp.bfloat16
BOTH = ("pa", "pb")
MIB = 1024 * 1024

KZ = np.array([j if j < 16 else j - 32 for j in range(32)])
KY = np.arange(16)


def split_table(table):
    high = jnp.asarray(table, F32).astype(B16)
    high = np.asarray(table, np.float32).astype(jnp.bfloat16)
    low = (np.asarray(table, np.float64) - high.astype(np.float64)).astype(jnp.bfloat16)
    return high, low


def rotation(angle, sign):
    cosine, sine = np.cos(angle), np.sin(angle)
    return np.stack([np.stack([cosine, -sign * sine]), np.stack([sign * sine, cosine])])


def tables():
    same_x = np.eye(4)
    angle = 2 * np.pi * (np.arange(NY)[:, None] * KY % NY) / NY
    y_part = np.stack([np.cos(angle), -np.sin(angle)], axis=1)
    y_forward = np.einsum("jJ,ypk->jyJpk", same_x, y_part).reshape(4, NY, 128)
    weight = np.where(KY == 0, 1.0, 2.0) / CELLS
    y_back = np.einsum("jJ,ypk,k->jpJky", same_x, y_part, weight).reshape(4, 128, NY)
    z = 4 * np.arange(16)[None, :] + np.arange(4)[:, None]
    angle = 2 * np.pi * (z[:, :, None] * KZ % NZ) / NZ
    z_forward = np.einsum("qpzaj,hH->pzhaqHj", rotation(angle, -1.0), np.eye(2)).reshape(256, 128)
    angle = 2 * np.pi * (z[:, :, None] * KZ % NZ) / NZ
    z_back = np.einsum("qpzaj->qzapj", rotation(angle, 1.0)).reshape(128, 64)
    return y_forward, y_back, z_forward, z_back


Y_FORWARD, Y_BACK, Z_FORWARD, Z_BACK = tables()
PHASE = np.stack([np.cos(2 * np.pi * np.arange(512) / 512), np.sin(2 * np.pi * np.arange(512) / 512)]).astype(np.float32)


def split(values):
    high = values.astype(B16)
    return high, (values - high.astype(F32)).astype(B16)


def dot(left, right):
    return jnp.dot(left, right, preferred_element_type=F32)


def dot_nt(left, right, precision=None):
    return lax.dot_general(left, right, (((1,), (1,)), ((), ())), precision=precision, preferred_element_type=F32)


def dot_exact(left, right):
    return jnp.dot(left, right, precision=EXACT, preferred_element_type=F32)


def iota(shape, axis):
    return lax.broadcasted_iota(jnp.int32, shape, axis)


def phase_index(frequency, block):
    return (frequency * (32 * block + 15)) & 511


def place(frequency):
    return (frequency % 32) // 2, frequency % 2


def cosine(frequency, step):
    return float(np.cos(2 * np.pi * frequency * (step + 0.5) / NX))


def sine(frequency, step):
    return float(np.sin(2 * np.pi * frequency * (step + 0.5) / NX))


def signs(rows, first):
    return jnp.where(iota((rows, 128), 1) < 64, first, -first).astype(F32)


def forward_kernel(
    phase_hbm, field_hbm, weight_hbm, y_hbm, out_ref, sent_ref, kept_ref,
    phase_ref, half_ref, rows_ref, field_ref, weight_ref, y_ref, sems,
):
    pa, pb = lax.axis_index("pa"), lax.axis_index("pb")
    copies = [
        pltpu.make_async_copy(source, target, sems.at[number])
        for number, (source, target) in enumerate(
            [
                (field_hbm.at[:, 0:128], field_ref.at[0]),
                (field_hbm.at[:, 128:256], field_ref.at[1]),
                (y_hbm, y_ref),
                (weight_hbm, weight_ref),
                (phase_hbm, phase_ref),
            ]
        )
    ]
    for copy in copies:
        copy.start()
    for copy in copies[0:3]:
        copy.wait()
    total = jnp.zeros((256, 128), F32)
    for xj in range(4):
        piece = jnp.concatenate(
            [field_ref[half, pl.ds(xj, 256, stride=4), :] for half in range(2)], axis=1
        )
        high, low = split(piece)
        product = dot(high, y_ref[xj])
        total = total + product[:, 0:128] + product[:, 128:256] + dot(low, y_ref[xj, :, 0:128])
    half_ref[...] = total
    copies[4].wait()
    lines = []
    for x4 in range(4):
        piece = jnp.concatenate([half_ref[pl.ds(z * 4 + x4, 16, stride=16), :] for z in range(4)], axis=0).T
        for xj in range(4):
            lines.append(jnp.concatenate([piece[32 * xj : 32 * xj + 16], piece[32 * xj + 16 : 32 * xj + 32]], axis=1))
    sign = signs(8, 1.0)
    for half in range(2):
        rows = slice(8 * half, 8 * half + 8)
        even = [lines[8 + j][rows] + lines[7 - j][rows] for j in range(8)]
        odd = [pltpu.roll(lines[8 + j][rows] - lines[7 - j][rows], 64, axis=1) * sign for j in range(8)]
        for frequency in range(17):
            first = sum(even[j] * cosine(frequency, j) for j in range(8))
            second = sum(odd[j] * sine(frequency, j) for j in range(8))
            values = {}
            if frequency < 16:
                values[frequency] = first + second
            if frequency > 0:
                values[-frequency] = first - second
            for signed, value in values.items():
                index = phase_index(signed, pb)
                kxp, kxl = place(signed)
                out_ref[pl.ds(kxp * 32 + kxl + 16 * half, 8, stride=2), :] = value * phase_ref[0, index] + pltpu.roll(
                    value, 64, axis=1
                ) * (sign * phase_ref[1, index])
    copies[3].wait()
    rows_ref[:, 0:32] = weight_ref[...]
    for target, wanted in ((sent_ref, jnp.where(pa < 8, 1, 0)), (kept_ref, 0)):
        chosen = rows_ref[pl.ds(wanted, 512, stride=2), :]
        target[...] = jnp.concatenate([chosen[128 * q : 128 * (q + 1), 0:32] for q in range(4)], axis=1)


def local_kernel(
    field_hbm, map_ref, base_ref, coef_ref, hidden_hbm, stat_hbm, kan_hbm, shift_hbm,
    field_ref, hidden_ref, stat_ref, kan_ref, shift_ref, sems, out_sems,
):
    copies = [
        pltpu.make_async_copy(field_hbm.at[:, 128 * half : 128 * half + 128], field_ref.at[half], sems.at[half])
        for half in range(2)
    ]
    for copy in copies:
        copy.start()
    last = coef_ref[:, 7, :]
    pieces = [coef_ref[:, basis, :] - last for basis in range(7)] + [base_ref[...]]
    high, low = split(jnp.concatenate(pieces, axis=1))
    kan_ref[0:16, 0:128] = high
    kan_ref[0:16, 128:256] = high
    kan_ref[16:32, 0:128] = low
    kan_ref[16:32, 128:256] = jnp.zeros((16, 128), B16)
    shift_ref[...] = jnp.broadcast_to(jnp.sum(last, axis=1, keepdims=True), (16, 128))
    outs = [
        pltpu.make_async_copy(source, target, out_sems.at[number])
        for number, (source, target) in enumerate(
            [(kan_ref, kan_hbm), (shift_ref, shift_hbm), (hidden_ref, hidden_hbm), (stat_ref, stat_hbm)]
        )
    ]
    outs[0].start()
    outs[1].start()
    high, low = split(map_ref[...])
    zero = jnp.zeros((16, 16), B16)
    maps = jnp.concatenate(
        [jnp.concatenate([high, high], axis=1), jnp.concatenate([low, zero], axis=1)], axis=0
    )
    for copy in copies:
        copy.wait()

    def step(x, total):
        for z in range(4):
            rows = pl.ds(z * 16 + x, 16, stride=64)
            high, low = split(jnp.concatenate([field_ref[half, rows, :] for half in range(2)], axis=1))
            both = dot(maps, jnp.concatenate([high, low], axis=0))
            value = both[0:16] + both[16:32]
            total = total + value
            start = pl.multiple_of(x * 64 + z * 16, 16)
            hidden_ref[pl.ds(start, 16), :] = value
        return total

    total = lax.fori_loop(0, 16, step, jnp.zeros((16, 256), F32), unroll=4)
    outs[2].start()
    mean = jnp.sum(total, axis=1, keepdims=True) * (1.0 / BLOCK_CELLS)

    def spread(part, total):
        for z in range(4):
            start = pl.multiple_of(part * 64 + z * 16, 16)
            away = hidden_ref[pl.ds(start, 16), :] - mean
            total = total + away * away
        return total

    total = lax.fori_loop(0, 16, spread, jnp.zeros((16, 256), F32), unroll=4)
    squares = jnp.sum(total, axis=1, keepdims=True)
    first = iota((16, 128), 1) == 0
    stat_ref[0:16, :] = jnp.where(first, mean, 0.0)
    stat_ref[16:32, :] = jnp.where(first, squares, 0.0)
    outs[3].start()
    for copy in outs:
        copy.wait()


def mix_kernel(
    phase_hbm, got_hbm, weight_hbm, partner_hbm, kept_hbm, map_hbm, stat_hbm, z_hbm, back_hbm, out_ref,
    phase_ref, got_ref, map_ref, z_ref, back_ref, rows_ref, weight_ref, partner_ref, stat_ref, both_ref, sems,
):
    pa, pb = lax.axis_index("pa"), lax.axis_index("pb")
    copies = [
        pltpu.make_async_copy(source, target, sems.at[number])
        for number, (source, target) in enumerate(
            [
                (got_hbm, got_ref),
                (z_hbm, z_ref),
                (map_hbm, map_ref),
                (weight_hbm, weight_ref),
                (stat_hbm, stat_ref),
                (back_hbm, back_ref),
                (phase_hbm, phase_ref),
                (partner_hbm, partner_ref),
            ]
        )
    ]
    for copy in copies[0:7]:
        copy.start()

    @pl.when(pa == 0)
    def _():
        pltpu.make_async_copy(kept_hbm, partner_ref, sems.at[7]).start()

    @pl.when(pa != 0)
    def _():
        copies[7].start()

    for copy in copies[0:3]:
        copy.wait()
    total = jnp.sum(got_ref[...].reshape(16, 4, 8, 128), axis=1)
    total = total + pltpu.roll(total, 4, axis=1)
    total = total + pltpu.roll(total, 2, axis=1)
    rows_ref[...] = total.reshape(128, 128)
    lines = jnp.concatenate([rows_ref[pl.ds(0, 16, stride=8), :], rows_ref[pl.ds(1, 16, stride=8), :]], axis=0)
    lines = lines.T
    lines = jnp.concatenate([lines[16 * q : 16 * (q + 1)] for q in range(8)], axis=1)
    modes = dot_exact(lines, z_ref[...])
    real = [modes[:, 32 * k : 32 * k + 32] for k in range(2)]
    imag = [modes[:, 64 + 32 * k : 96 + 32 * k] for k in range(2)]
    lower = pa < 8
    far_real = jnp.where(lower, real[0], real[1])
    far_imag = jnp.where(lower, imag[0], imag[1])
    odd = iota((32, 32), 0) % 2 == 1
    twice = (iota((32, 16), 0) // 2 == iota((32, 16), 1)).astype(F32)
    map_rows = dot_exact(twice, map_ref[...])
    mixed_real = jnp.zeros((32, 32), F32)
    mixed_imag = jnp.zeros((32, 32), F32)
    local_real = jnp.zeros((32, 32), F32)
    local_imag = jnp.zeros((32, 32), F32)
    partner_real = jnp.zeros((32, 32), F32)
    partner_imag = jnp.zeros((32, 32), F32)
    for copy in copies[3:8]:
        copy.wait()
    source, target = iota((128, 128), 0), iota((128, 128), 1)
    turn = jnp.logical_and(source // 32 == target // 32, source % 32 == (32 - target % 32) % 32)
    turn = jnp.logical_and(turn, target % 32 != 16).astype(F32)
    turned = dot_exact(partner_ref[...], turn)
    both_ref[pl.ds(0, 128, stride=2), :] = turned
    both_ref[pl.ds(1, 128, stride=2), :] = turned
    for i in range(16):
        mode_real = jnp.where(odd, real[1][i : i + 1], real[0][i : i + 1])
        mode_imag = jnp.where(odd, imag[1][i : i + 1], imag[0][i : i + 1])
        weight_real = weight_ref[32 * i : 32 * i + 32, :]
        weight_imag = weight_ref[512 + 32 * i : 544 + 32 * i, :]
        mixed_real = mixed_real + weight_real * mode_real - weight_imag * mode_imag
        mixed_imag = mixed_imag + weight_real * mode_imag + weight_imag * mode_real
        column = map_rows[:, i : i + 1]
        local_real = local_real + column * mode_real
        local_imag = local_imag + column * mode_imag
        row = 32 * (i % 8)
        lane = 32 * (i // 8)
        weight_real = both_ref[row : row + 32, lane : lane + 32]
        weight_imag = both_ref[row : row + 32, 64 + lane : 96 + lane]
        mode_real = far_real[i : i + 1]
        mode_imag = far_imag[i : i + 1]
        partner_real = partner_real + weight_real * mode_real + weight_imag * mode_imag
        partner_imag = partner_imag + weight_imag * mode_real - weight_real * mode_imag
    origin = jnp.logical_and(
        jnp.logical_and(pa == 0, pb == 0), jnp.logical_and(iota((32, 32), 0) % 2 == 0, iota((32, 32), 1) == 0)
    )
    centre = jnp.where(origin, mixed_real, 0.0)
    moved_real = jnp.where(origin, 0.0, mixed_real)
    moved_imag = jnp.where(origin, 0.0, mixed_imag)
    own = jnp.where(pb == 0, 0.5, 2.0)
    cross = jnp.where(pb == 0, 2.0, 4.0)
    power = own * (moved_real * moved_real + moved_imag * moved_imag)
    power = power + cross * (moved_real * local_real + moved_imag * local_imag)
    pair = moved_real * partner_real - moved_imag * partner_imag
    chosen = jnp.where(lower, 0, 1)
    pair = jnp.where(
        jnp.logical_and(pb == 0, iota((32, 32), 0) % 2 == chosen), jnp.where(pa == 0, 0.5, 1.0) * pair, 0.0
    )
    power = power + pair
    sums = jnp.concatenate(
        [
            power * (1.0 / CELLS),
            jnp.zeros((16, 32), F32),
            stat_ref[:, 0:32],
            centre * (1.0 / CELLS),
            jnp.zeros((16, 32), F32),
        ],
        axis=0,
    )
    sums = dot_nt(jnp.ones((8, 32), F32), sums, EXACT)
    out_ref[pl.ds(2, 256, stride=3), :] = jnp.broadcast_to(sums[0:1], (256, 128))
    order = (iota((32, 32), 1) == 2 * (iota((32, 32), 0) % 16) + iota((32, 32), 0) // 16).astype(F32)
    mixed = dot_exact(order, jnp.concatenate([mixed_real, mixed_imag], axis=1))
    planes = dot_nt(back_ref[...], mixed, EXACT)
    sign = signs(16, -1.0)
    for kxl in range(2):
        frequency = 2 * pa + kxl - jnp.where(lower, 0, 32)
        value = jnp.concatenate(
            [planes[16 * q : 16 * (q + 1), 16 * kxl : 16 * kxl + 16] for q in range(8)], axis=1
        )
        other = pltpu.roll(value, 64, axis=1) * sign
        for block in range(16):
            index = phase_index(frequency, block)
            out_ref[pl.ds(block * 3 + kxl, 16, stride=48), :] = (
                value * phase_ref[0, index] + other * phase_ref[1, index]
            )


def column(row):
    eye = (iota((16, 16), 0) == iota((16, 16), 1)).astype(F32)
    return dot_nt(eye, jnp.broadcast_to(row, (8, 16)), EXACT)[:, 0:1]


def output_kernel(
    got_hbm, hidden_hbm, index_hbm, kan_hbm, constant_hbm, gain_hbm, bias_hbm,
    y_high_hbm, y_low_hbm, out_ref,
    gain_ref, bias_ref, got_ref, y_high_ref, y_low_ref,
    spec_ref, result_ref, hidden_ref, index_ref, kan_ref, constant_ref, in_sems, sems,
):
    reads = [
        pltpu.make_async_copy(source, target, in_sems.at[number])
        for number, (source, target) in enumerate(
            [
                (got_hbm, got_ref),
                (gain_hbm, gain_ref),
                (bias_hbm, bias_ref),
                (y_high_hbm, y_high_ref),
                (y_low_hbm, y_low_ref),
                (kan_hbm, kan_ref),
                (constant_hbm, constant_ref),
                (hidden_hbm.at[:, 0:128], hidden_ref.at[:, 0:128]),
                (index_hbm.at[:, 0:128], index_ref.at[0]),
                (hidden_hbm.at[:, 128:256], hidden_ref.at[:, 128:256]),
                (index_hbm.at[:, 128:256], index_ref.at[1]),
            ]
        )
    ]
    for copy in reads[0:5]:
        copy.start()
    for copy in reads[0:3]:
        copy.wait()
    for copy in reads[5:11]:
        copy.start()
    stats = got_ref[pl.ds(2, 256, stride=3), :]
    sums = jnp.sum(stats, axis=0, keepdims=True)
    mean = sums * (1.0 / 256)
    away = stats - mean
    between = jnp.sum(away * away, axis=0, keepdims=True) * float(BLOCK_CELLS)
    lane = iota((1, 128), 1)
    is_mean = jnp.logical_and(lane >= 48, lane < 64)
    is_centre = jnp.logical_and(lane >= 80, lane < 112)
    variance = jnp.where(is_mean, between, jnp.where(lane < 80, sums, 0.0)) * (1.0 / CELLS)
    mean = jnp.where(is_mean, mean, jnp.where(is_centre, sums, 0.0))
    lane, row = iota((16, 128), 1), iota((16, 128), 0)
    owner = jnp.where(
        lane < 32, lane // 2, jnp.where(lane < 80, lane % 16, jnp.where(lane < 112, (lane - 80) // 2, -1))
    )
    pick = (owner == row).astype(F32)
    mean = dot_nt(pick, jnp.broadcast_to(mean, (8, 128)), EXACT)[:, 0:1]
    variance = dot_nt(pick, jnp.broadcast_to(variance, (8, 128)), EXACT)[:, 0:1]
    scale = column(gain_ref[...]) * lax.rsqrt(variance + EPSILON)
    mean = jnp.broadcast_to(jnp.concatenate([mean] * 4, axis=0), (64, 128))
    scale = jnp.broadcast_to(jnp.concatenate([scale] * 4, axis=0), (64, 128))
    bias = jnp.broadcast_to(jnp.concatenate([column(bias_ref[...])] * 4, axis=0), (64, 128))
    lines = [[None] * 2 for _ in range(16)]
    sign = signs(8, -1.0)
    for half in range(2):
        modes = {}
        for frequency in range(-16, 16):
            kxp, kxl = place(frequency)
            modes[frequency] = got_ref[pl.ds(kxp * 48 + kxl + 24 * half, 8, stride=3), :]
        even = [modes[k] + modes[-k] for k in range(1, 16)] + [modes[-16]]
        odd = [modes[k] - modes[-k] for k in range(1, 16)] + [-modes[-16]]
        odd = [pltpu.roll(value, 64, axis=1) * sign for value in odd]
        for j in range(8):
            first = modes[0] + sum(even[k - 1] * cosine(k, j) for k in range(1, 17))
            second = sum(odd[k - 1] * sine(k, j) for k in range(1, 17))
            lines[8 + j][half] = first + second
            lines[7 - j][half] = first - second
    groups = []
    for x4 in range(4):
        piece = jnp.concatenate([lines[4 * x4 + xj][half] for xj in range(4) for half in range(2)], axis=0).T
        groups.append(jnp.concatenate([piece[0:64], piece[64:128]], axis=1))
    high, low = split(jnp.concatenate(groups, axis=0))
    both = jnp.concatenate([high, low], axis=0)
    reads[3].wait()
    reads[4].wait()
    for xj in range(4):
        product = dot(both, y_high_ref[xj])
        value = product[0:256] + product[256:512] + dot(high, y_low_ref[xj])
        for x4 in range(4):
            start = (4 * x4 + xj) * 64
            spec_ref[start : start + 64, :] = value[64 * x4 : 64 * x4 + 64]
    for copy in reads[5:9]:
        copy.wait()
    weights = kan_ref[...]
    constant = constant_ref[...]
    copies = []
    for half in range(2):
        lanes = slice(128 * half, 128 * half + 128)
        if half == 1:
            reads[9].wait()
            reads[10].wait()

        def step(x, carry, half=half, lanes=lanes):
            rows = pl.ds(pl.multiple_of(x * 64, 64), 64)
            hidden = spec_ref[rows, lanes] + hidden_ref[rows, lanes]
            normed = (hidden - mean) * scale + bias
            level = jnp.concatenate(
                [index_ref[half, pl.ds(z * 16 + x, 16, stride=64), :] for z in range(4)], axis=0
            ).astype(F32)
            local = jnp.clip(normed * 1.25 + (2.5 - level), 0.0, 1.0)
            other = 1.0 - local
            square = local * local
            cube = square * local
            p0 = other * other * other * (1.0 / 6.0)
            p3 = cube * (1.0 / 6.0)
            p1 = 0.5 * cube - square + 2.0 / 3.0
            p2 = 0.5 * (square + local - cube) + 1.0 / 6.0
            level = level.astype(B16)
            at = [level == jnp.asarray(k, B16) for k in range(5)]
            zero = jnp.zeros((64, 128), B16)
            pieces = [split(piece) for piece in (p0, p1, p2, p3)]
            parts = []
            for basis in range(7):
                value = [zero, zero]
                for r in range(4):
                    if 0 <= basis - r <= 4:
                        value = [jnp.where(at[basis - r], pieces[r][k], value[k]) for k in range(2)]
                parts.append(value)
            parts.append(split(0.5 * normed * (1.0 + jnp.tanh(0.5 * normed))))
            columns = []
            for z in range(4):
                columns.append(
                    jnp.concatenate(
                        [part[0][16 * z : 16 * z + 16] for part in parts]
                        + [part[1][16 * z : 16 * z + 16] for part in parts],
                        axis=0,
                    )
                )
            product = dot(weights, jnp.concatenate(columns, axis=1))
            for z in range(4):
                value = product[0:16, 128 * z : 128 * z + 128] + product[16:32, 128 * z : 128 * z + 128]
                result_ref[half, pl.ds(z * 16 + x, 16, stride=64), :] = value + constant
            return carry

        for part in range(2):
            lax.fori_loop(8 * part, 8 * part + 8, step, 0, unroll=8)
            copy = pltpu.make_async_copy(
                result_ref.at[half].reshape(64, 16, 128).at[:, 8 * part : 8 * part + 8, :],
                out_ref.at[:, 8 * part : 8 * part + 8, lanes],
                sems.at[2 * half + part],
            )
            copy.start()
            copies.append(copy)
    for copy in copies:
        copy.wait()


def whole():
    return pl.BlockSpec(memory_space=pltpu.VMEM)


def scalars():
    return pl.BlockSpec(memory_space=pltpu.SMEM)


def hbm():
    return pl.BlockSpec(memory_space=pltpu.HBM)


def params(vmem):
    return pltpu.CompilerParams(vmem_limit_bytes=vmem * MIB)


def cost(flops, moved):
    return pl.CostEstimate(flops=flops, bytes_accessed=moved, transcendentals=0)


def shape(dims, dtype=F32):
    return jax.ShapeDtypeStruct(dims, dtype)


def transfers(count):
    return pltpu.SemaphoreType.DMA((count,))


def forward_call(field, weight):
    y_high, y_low = split_table(Y_FORWARD)
    return pl.pallas_call(
        forward_kernel,
        out_shape=(shape((512, 128)), shape((128, 128)), shape((128, 128))),
        in_specs=[hbm()] * 4,
        out_specs=(whole(),) * 3,
        scratch_shapes=[
            pltpu.SMEM((2, 512), F32),
            pltpu.VMEM((256, 128), F32),
            pltpu.VMEM((1024, 128), F32),
            pltpu.VMEM((2, 1024, 128), F32),
            pltpu.VMEM((1024, 32), F32),
            pltpu.VMEM((4, 256, 256), B16),
            transfers(5),
        ],
        compiler_params=params(60),
        cost_estimate=cost(4 * 10**8, 4 * 10**6),
        name="forward",
    )(
        jnp.asarray(PHASE), field, weight,
        jnp.asarray(np.concatenate([y_high, y_low], axis=2)),
    )


def local_call(field, local_weight, base_weight, spline_coef):
    return pl.pallas_call(
        local_kernel,
        out_shape=(shape((1024, 256)), shape((32, 128)), shape((32, 256), B16), shape((16, 128))),
        in_specs=[hbm()] + [whole()] * 3,
        out_specs=(hbm(),) * 4,
        scratch_shapes=[
            pltpu.VMEM((2, 1024, 128), F32),
            pltpu.VMEM((1024, 256), F32),
            pltpu.VMEM((32, 128), F32),
            pltpu.VMEM((32, 256), B16),
            pltpu.VMEM((16, 128), F32),
            transfers(2),
            transfers(4),
        ],
        compiler_params=params(60),
        cost_estimate=cost(10**8, 2 * 10**6),
        name="local",
    )(field, local_weight, base_weight, jnp.transpose(spline_coef, (0, 2, 1)))


def mix_call(got, weight, partner, kept, local_weight, stat):
    return pl.pallas_call(
        mix_kernel,
        out_shape=shape((768, 128)),
        in_specs=[hbm()] * 9,
        out_specs=whole(),
        scratch_shapes=[
            pltpu.SMEM((2, 512), F32),
            pltpu.VMEM((512, 128), F32),
            pltpu.VMEM((16, 16), F32),
            pltpu.VMEM((256, 128), F32),
            pltpu.VMEM((128, 64), F32),
            pltpu.VMEM((128, 128), F32),
            pltpu.VMEM((1024, 32), F32),
            pltpu.VMEM((128, 128), F32),
            pltpu.VMEM((32, 128), F32),
            pltpu.VMEM((256, 128), F32),
            transfers(8),
        ],
        compiler_params=params(60),
        cost_estimate=cost(10**7, 10**6),
        name="mix",
    )(
        jnp.asarray(PHASE), got, weight, partner, kept, local_weight, stat,
        jnp.asarray(Z_FORWARD, F32), jnp.asarray(Z_BACK, F32),
    )


def output_call(back, hidden, index, kan, constant, bn_gain, bn_shift):
    y_high, y_low = split_table(Y_BACK)
    return pl.pallas_call(
        output_kernel,
        out_shape=shape((64, 16, 256)),
        in_specs=[hbm()] * 9,
        out_specs=hbm(),
        scratch_shapes=[
            pltpu.VMEM((1, 16), F32),
            pltpu.VMEM((1, 16), F32),
            pltpu.VMEM((768, 128), F32),
            pltpu.VMEM((4, 128, 256), B16),
            pltpu.VMEM((4, 128, 256), B16),
            pltpu.VMEM((1024, 256), F32),
            pltpu.VMEM((2, 1024, 128), F32),
            pltpu.VMEM((1024, 256), F32),
            pltpu.VMEM((2, 1024, 128), jnp.int32),
            pltpu.VMEM((32, 256), B16),
            pltpu.VMEM((16, 128), F32),
            transfers(11),
            transfers(4),
        ],
        compiler_params=params(60),
        cost_estimate=cost(10**9, 6 * 10**6),
        name="output",
    )(
        back, hidden, index, kan, constant, bn_gain.reshape(1, 16), bn_shift.reshape(1, 16),
        jnp.asarray(y_high), jnp.asarray(y_low),
    )


def on_device(
    field, spline_index, spec_weight, local_weight, bn_gain, bn_shift, base_weight, spline_coef
):
    field = field.reshape(1024, 256)
    index = spline_index.reshape(1024, 256)
    weight = jnp.transpose(spec_weight, (0, 1, 2, 4, 5, 3)).reshape(1024, 32)
    sent, own, kept = forward_call(field, weight)
    path = [0]
    while path[-1] != 8:
        path.append(15 - path[-1] if path[-1] < 8 else 16 - path[-1])
    partner = lax.ppermute(own, BOTH, [(16 * a, 16 * b) for a, b in zip(path[:-1], path[1:])])
    got = lax.all_to_all(sent.reshape(256, 2, 128), BOTH, 0, 0, tiled=True).reshape(512, 128)
    hidden, stat, kan, constant = local_call(field, local_weight, base_weight, spline_coef)
    back = mix_call(got, weight, partner, kept, local_weight, stat)
    back = lax.all_to_all(back.reshape(256, 1, 384), BOTH, 0, 0, tiled=True).reshape(768, 128)
    output = output_call(back, hidden, index, kan, constant, bn_gain, bn_shift)
    return output.reshape(16, 4, 16, 256)


def solution(mesh):
    in_specs = (
        P(None, "pa", "pb", None),
        P(None, "pa", "pb", None),
        P(None, None, None, None, "pa", "pb"),
        P(),
        P(),
        P(),
        P(),
        P(),
    )
    out_specs = P(None, "pa", "pb", None)
    return jax.shard_map(
        on_device, mesh=mesh, in_specs=in_specs, out_specs=out_specs, check_vma=False
    )
```

time: 83.8 us -> 72.1 us (0.86)
  Pallas kernels: 26.8 us -> 18.3 us
  local copies, waits for them, and re-layouts: 2.78 us -> 0.71 us
  blocking collectives: 27 us -> 25.9 us
    pallas_call x4, Pallas kernels: 26.8 us -> 18.3 us  [the longest x1 7.05 us: output_call(): pl.pallas_call(output_kernel, out_shape=shape((64, 16, 256)), in_specs=[h...]
    reshape x2 -> x0, local copies, waits for them, and re-layouts: 2.08 us -> none  [the longest x1 1.16 us: on_device(): back.reshape(256, 3, 128)]
    all_to_all x1, blocking collectives: 27 us -> 25.9 us  [on_device(): lax.all_to_all(back.reshape(256, 1, 384), BOTH, 0, 0, tiled=True)]
  transfers between devices with their start and end apart: 2 -> 2, of which waited for: 0 -> 1; matrix products, arithmetic and copies ran while one was open for 0% -> 0% of each run, Pallas kernels for 7% -> 6%
where the time goes in v2:
time: 72.1 us; the launch traced here: 71.7 us
  starting transfers between devices  26.4 us (37%)
  blocking collectives  25.9 us (36%)
  Pallas kernels  18.3 us (25%)
    all_to_all x1, blocking collectives, on_device(): lax.all_to_all(back.reshape(256, 1, 384), BOTH, 0, 0, tiled=True)  25.9 us
    all_to_all x1, starting transfers between devices, on_device(): lax.all_to_all(sent.reshape(256, 2, 128), BOTH, 0, 0, tiled=True)  15.7 us
    ppermute x1, starting transfers between devices, on_device(): lax.ppermute(own, BOTH, [(16 * a, 16 * b) for a, b in zip(path[:-1], path...  10.7 us
    pallas_call x1, Pallas kernels, output_call(): pl.pallas_call(output_kernel, out_shape=shape((64, 16, 256)), in_specs=[h...  7.05 us
    pallas_call x1, Pallas kernels, local_call(): pl.pallas_call(local_kernel, out_shape=(shape((1024, 256)), shape((32, 12...  4.25 us
    pallas_call x1, Pallas kernels, mix_call(): pl.pallas_call(mix_kernel, out_shape=shape((768, 128)), in_specs=[hbm()]...  3.69 us
    pallas_call x1, Pallas kernels, forward_call(): pl.pallas_call(forward_kernel, out_shape=(shape((512, 128)), shape((128,...  3.29 us
  transfers between devices with their start and end apart: 2, of which 1 were waited for; matrix products, arithmetic and copies ran while one was open for 0% of the time, Pallas kernels for 6%

profile of v2, /device:TPU:1, one launch (start us, length us, event | category | flops | bytes accessed | tf_op | source)
XLA Modules:
  0.0 71.7 jit_solution(16019819810709802763)
XLA Ops:
  0.0 3.3 %forward.1 = (f32[512,128]{1,0:T(8,128)}, f32[128,128]{1,0:T(8,128)}, f32[128,128]{1,0:T(8,128)}) custom-call(f32[2,512]{1,0:T(2,128)} %constant.12.clone.phase_hbm, f32[1024,256]{1,0:T(8,128)} %bitcast.13, f32[1024,32]{1,0:T(8,128)} %bitcast.15, bf16[4,256,256]{2,1,0:T(8,128)(2,1)} %constant.13.clone.y_hbm), custom_call_target="tpu_custom_call" | custom-call | flops 400000000 | bytes 4000000 | tf_op jit(solution)/shard_map/forward/pallas_call | solution.py:530
  3.3 0.0 copy-start.2
  3.3 15.7 %all-to-all-start = ((f32[256,2,128]{2,1,0:T(2,128)}), f32[256,2,128]{2,1,0:T(2,128)S(1)}, u32[]{:S(2)}, u32[]{:S(2)}) async-start(f32[256,2,128]{2,1,0:T(2,128)} %bitcast.21), calls=%async_computation | async-start | bytes 524288 | tf_op jit(solution)/shard_map/all_to_all | solution.py:644
  19.0 0.0 copy-done.2
  19.0 10.7 %collective-permute-start = (f32[128,128]{1,0:T(8,128)S(1)}, f32[128,128]{1,0:T(8,128)S(1)}, u32[]{:S(2)}, u32[]{:S(2)}) collective-permute-start(f32[128,128]{1,0:T(8,128)S(1)} %copy-done.2), channel_id=1, source_target_pairs={{0,240},{240,16},{16,224},{224,32},{32,208},{208,48},{48,192},{192... | collective-permute-start | bytes 196616 | tf_op jit(solution)/shard_map/ppermute | solution.py:643
  29.7 4.2 %local.1 = (f32[1024,256]{1,0:T(8,128)}, f32[32,128]{1,0:T(8,128)}, bf16[32,256]{1,0:T(8,128)(2,1)}, f32[16,128]{1,0:T(8,128)}) custom-call(f32[1024,256]{1,0:T(8,128)} %bitcast.14, f32[16,16]{1,0:T(8,128)} %map_hbm.1, f32[16,16]{1,0:T(8,128)} %base_ref.1, f32[16,8,16]{2,1,0:T(8,128)} %bitcast.22), custom_call_target="tpu_custom_call" | custom-call | flops 100000000 | bytes 2000000 | tf_op jit(solution)/shard_map/local/pallas_call | solution.py:554
  34.0 0.0 collective-permute-done.partner_hbm
  34.0 0.0 copy-start.1
  34.0 0.4 all-to-all-done
  34.4 0.0 copy-start
  34.4 0.2 copy-done.1
  34.6 0.5 copy-done
  35.1 3.7 %mix.1 = f32[768,128]{1,0:T(8,128)} custom-call(f32[2,512]{1,0:T(2,128)} %constant.12.clone.phase_hbm, f32[512,128]{1,0:T(8,128)} %bitcast.20, f32[1024,32]{1,0:T(8,128)} %bitcast.16, f32[128,128]{1,0:T(8,128)} %copy-done.1, f32[128,128]{1,0:T(8,128)} %get-tuple-element.14.kept_hbm, f32[16,16]{1,0:T(8,128)} %map_hbm.1, ...), custom_call_target="tpu_custom_call" | custom-call | flops 10000000 | bytes 1000000 | tf_op jit(solution)/shard_map/mix/pallas_call | solution.py:575
  38.8 25.9 %all_to_all.10 = f32[256,1,384]{2,1,0:T(1,128)} all-to-all(f32[256,1,384]{2,1,0:T(1,128)} %bitcast.18), channel_id=1, replica_groups=mesh['pa'=16,'pb'=16] {'pa','pb'}, dimensions={0} | all-to-all | bytes 786432 | tf_op jit(solution)/shard_map/all_to_all | solution.py:647
  64.7 7.0 %output.1 = f32[64,16,256]{2,1,0:T(8,128)} custom-call(f32[768,128]{1,0:T(8,128)} %bitcast.17, f32[1024,256]{1,0:T(8,128)} %get-tuple-element.16.hidden_hbm, s32[1024,256]{1,0:T(8,128)} %bitcast.19, bf16[32,256]{1,0:T(8,128)(2,1)} %get-tuple-element.17.kan_hbm, f32[16,128]{1,0:T(8,128)} %get-tuple-element.18.constant_hbm, f32[1,16]{1,0:T(1,128)} %bitcast.23, ...), custom_call_target="tpu_custom_call" | custom-call | flops 1000000000 | bytes 6000000 | tf_op jit(solution)/shard_map/output/pallas_call | solution.py:604
Async XLA Ops:
  3.3 15.7 %copy-start.2 = (f32[128,128]{1,0:T(8,128)S(1)}, f32[128,128]{1,0:T(8,128)}, u32[]{:S(2)}) copy-start(f32[128,128]{1,0:T(8,128)} %get-tuple-element.13) | copy-start | bytes 196612
  3.3 31.1 %all-to-all-start = ((f32[256,2,128]{2,1,0:T(2,128)}), f32[256,2,128]{2,1,0:T(2,128)S(1)}, u32[]{:S(2)}, u32[]{:S(2)}) async-start(f32[256,2,128]{2,1,0:T(2,128)} %bitcast.21), calls=%async_computation | async-start | bytes 524288 | tf_op jit(solution)/shard_map/all_to_all | solution.py:644
  19.0 15.0 %collective-permute-start = (f32[128,128]{1,0:T(8,128)S(1)}, f32[128,128]{1,0:T(8,128)S(1)}, u32[]{:S(2)}, u32[]{:S(2)}) collective-permute-start(f32[128,128]{1,0:T(8,128)S(1)} %copy-done.2), channel_id=1, source_target_pairs={{0,240},{240,16},{16,224},{224,32},{32,208},{208,48},{48,192},{192... | collective-permute-start | bytes 196616 | tf_op jit(solution)/shard_map/ppermute | solution.py:643
  34.0 0.6 copy-start.1
  34.4 0.7 copy-start

commit v3 on v2

--- a/solution.py
+++ b/solution.py
@@ -15,6 +15,7 @@
 B16 = jnp.bfloat16
 BOTH = ("pa", "pb")
 MIB = 1024 * 1024
+PITCH = 72
 
 KZ = np.array([j if j < 16 else j - 32 for j in range(32)])
 KY = np.arange(16)
@@ -155,15 +156,25 @@
 
 
 def local_kernel(
-    field_hbm, map_ref, base_ref, coef_ref, hidden_hbm, stat_hbm, kan_hbm, shift_hbm,
-    field_ref, hidden_ref, stat_ref, kan_ref, shift_ref, sems, out_sems,
+    field_hbm, map_hbm, base_hbm, coef_hbm, hidden_hbm, stat_ref, kan_hbm, shift_hbm,
+    map_ref, base_ref, coef_ref, field_ref, hidden_ref, kan_ref, shift_ref, sems, out_sems,
 ):
     copies = [
-        pltpu.make_async_copy(field_hbm.at[:, 128 * half : 128 * half + 128], field_ref.at[half], sems.at[half])
+        pltpu.make_async_copy(
+            field_hbm.at[:, :, 128 * half : 128 * half + 128],
+            field_ref.at[half].reshape(16, PITCH, 128).at[:, 0:64, :],
+            sems.at[half],
+        )
         for half in range(2)
     ]
-    for copy in copies:
+    small = [
+        pltpu.make_async_copy(source, target, sems.at[2 + number])
+        for number, (source, target) in enumerate([(map_hbm, map_ref), (base_hbm, base_ref), (coef_hbm, coef_ref)])
+    ]
+    for copy in small + copies:
         copy.start()
+    for copy in small:
+        copy.wait()
     last = coef_ref[:, 7, :]
     pieces = [coef_ref[:, basis, :] - last for basis in range(7)] + [base_ref[...]]
     high, low = split(jnp.concatenate(pieces, axis=1))
@@ -175,7 +186,7 @@
     outs = [
         pltpu.make_async_copy(source, target, out_sems.at[number])
         for number, (source, target) in enumerate(
-            [(kan_ref, kan_hbm), (shift_ref, shift_hbm), (hidden_ref, hidden_hbm), (stat_ref, stat_hbm)]
+            [(kan_ref, kan_hbm), (shift_ref, shift_hbm), (hidden_ref, hidden_hbm)]
         )
     ]
     outs[0].start()
@@ -190,7 +201,7 @@
 
     def step(x, total):
         for z in range(4):
-            rows = pl.ds(z * 16 + x, 16, stride=64)
+            rows = pl.ds(z * 16 + x, 16, stride=PITCH)
             high, low = split(jnp.concatenate([field_ref[half, rows, :] for half in range(2)], axis=1))
             both = dot(maps, jnp.concatenate([high, low], axis=0))
             value = both[0:16] + both[16:32]
@@ -215,44 +226,29 @@
     first = iota((16, 128), 1) == 0
     stat_ref[0:16, :] = jnp.where(first, mean, 0.0)
     stat_ref[16:32, :] = jnp.where(first, squares, 0.0)
-    outs[3].start()
     for copy in outs:
         copy.wait()
 
 
 def mix_kernel(
-    phase_hbm, got_hbm, weight_hbm, partner_hbm, kept_hbm, map_hbm, stat_hbm, z_hbm, back_hbm, out_ref,
-    phase_ref, got_ref, map_ref, z_ref, back_ref, rows_ref, weight_ref, partner_ref, stat_ref, both_ref, sems,
+    got_ref, partner_ref, kept_ref, stat_ref, phase_hbm, weight_hbm, map_hbm, z_hbm, back_hbm, out_ref,
+    phase_ref, map_ref, z_ref, back_ref, rows_ref, weight_ref, both_ref, sems,
 ):
     pa, pb = lax.axis_index("pa"), lax.axis_index("pb")
     copies = [
         pltpu.make_async_copy(source, target, sems.at[number])
         for number, (source, target) in enumerate(
             [
-                (got_hbm, got_ref),
                 (z_hbm, z_ref),
                 (map_hbm, map_ref),
                 (weight_hbm, weight_ref),
-                (stat_hbm, stat_ref),
                 (back_hbm, back_ref),
                 (phase_hbm, phase_ref),
-                (partner_hbm, partner_ref),
             ]
         )
     ]
-    for copy in copies[0:7]:
+    for copy in copies:
         copy.start()
-
-    @pl.when(pa == 0)
-    def _():
-        pltpu.make_async_copy(kept_hbm, partner_ref, sems.at[7]).start()
-
-    @pl.when(pa != 0)
-    def _():
-        copies[7].start()
-
-    for copy in copies[0:3]:
-        copy.wait()
     total = jnp.sum(got_ref[...].reshape(16, 4, 8, 128), axis=1)
     total = total + pltpu.roll(total, 4, axis=1)
     total = total + pltpu.roll(total, 2, axis=1)
@@ -260,6 +256,8 @@
     lines = jnp.concatenate([rows_ref[pl.ds(0, 16, stride=8), :], rows_ref[pl.ds(1, 16, stride=8), :]], axis=0)
     lines = lines.T
     lines = jnp.concatenate([lines[16 * q : 16 * (q + 1)] for q in range(8)], axis=1)
+    for copy in copies:
+        copy.wait()
     modes = dot_exact(lines, z_ref[...])
     real = [modes[:, 32 * k : 32 * k + 32] for k in range(2)]
     imag = [modes[:, 64 + 32 * k : 96 + 32 * k] for k in range(2)]
@@ -275,12 +273,10 @@
     local_imag = jnp.zeros((32, 32), F32)
     partner_real = jnp.zeros((32, 32), F32)
     partner_imag = jnp.zeros((32, 32), F32)
-    for copy in copies[3:8]:
-        copy.wait()
     source, target = iota((128, 128), 0), iota((128, 128), 1)
     turn = jnp.logical_and(source // 32 == target // 32, source % 32 == (32 - target % 32) % 32)
     turn = jnp.logical_and(turn, target % 32 != 16).astype(F32)
-    turned = dot_exact(partner_ref[...], turn)
+    turned = dot_exact(jnp.where(pa == 0, kept_ref[...], partner_ref[...]), turn)
     both_ref[pl.ds(0, 128, stride=2), :] = turned
     both_ref[pl.ds(1, 128, stride=2), :] = turned
     for i in range(16):
@@ -352,16 +348,15 @@
 
 
 def output_kernel(
-    got_hbm, hidden_hbm, index_hbm, kan_hbm, constant_hbm, gain_hbm, bias_hbm,
+    got_ref, hidden_hbm, index_hbm, kan_hbm, constant_hbm, gain_hbm, bias_hbm,
     y_high_hbm, y_low_hbm, out_ref,
-    gain_ref, bias_ref, got_ref, y_high_ref, y_low_ref,
+    gain_ref, bias_ref, y_high_ref, y_low_ref,
     spec_ref, result_ref, hidden_ref, index_ref, kan_ref, constant_ref, in_sems, sems,
 ):
     reads = [
         pltpu.make_async_copy(source, target, in_sems.at[number])
         for number, (source, target) in enumerate(
             [
-                (got_hbm, got_ref),
                 (gain_hbm, gain_ref),
                 (bias_hbm, bias_ref),
                 (y_high_hbm, y_high_ref),
@@ -369,17 +364,13 @@
                 (kan_hbm, kan_ref),
                 (constant_hbm, constant_ref),
                 (hidden_hbm.at[:, 0:128], hidden_ref.at[:, 0:128]),
-                (index_hbm.at[:, 0:128], index_ref.at[0]),
+                (index_hbm.at[:, :, 0:128], index_ref.at[0].reshape(16, PITCH, 128).at[:, 0:64, :]),
                 (hidden_hbm.at[:, 128:256], hidden_ref.at[:, 128:256]),
-                (index_hbm.at[:, 128:256], index_ref.at[1]),
+                (index_hbm.at[:, :, 128:256], index_ref.at[1].reshape(16, PITCH, 128).at[:, 0:64, :]),
             ]
         )
     ]
-    for copy in reads[0:5]:
-        copy.start()
-    for copy in reads[0:3]:
-        copy.wait()
-    for copy in reads[5:11]:
+    for copy in reads:
         copy.start()
     stats = got_ref[pl.ds(2, 256, stride=3), :]
     sums = jnp.sum(stats, axis=0, keepdims=True)
@@ -398,6 +389,8 @@
     pick = (owner == row).astype(F32)
     mean = dot_nt(pick, jnp.broadcast_to(mean, (8, 128)), EXACT)[:, 0:1]
     variance = dot_nt(pick, jnp.broadcast_to(variance, (8, 128)), EXACT)[:, 0:1]
+    reads[0].wait()
+    reads[1].wait()
     scale = column(gain_ref[...]) * lax.rsqrt(variance + EPSILON)
     mean = jnp.broadcast_to(jnp.concatenate([mean] * 4, axis=0), (64, 128))
     scale = jnp.broadcast_to(jnp.concatenate([scale] * 4, axis=0), (64, 128))
@@ -423,15 +416,15 @@
         groups.append(jnp.concatenate([piece[0:64], piece[64:128]], axis=1))
     high, low = split(jnp.concatenate(groups, axis=0))
     both = jnp.concatenate([high, low], axis=0)
+    reads[2].wait()
     reads[3].wait()
-    reads[4].wait()
     for xj in range(4):
         product = dot(both, y_high_ref[xj])
         value = product[0:256] + product[256:512] + dot(high, y_low_ref[xj])
         for x4 in range(4):
             start = (4 * x4 + xj) * 64
             spec_ref[start : start + 64, :] = value[64 * x4 : 64 * x4 + 64]
-    for copy in reads[5:9]:
+    for copy in reads[4:8]:
         copy.wait()
     weights = kan_ref[...]
     constant = constant_ref[...]
@@ -439,15 +432,15 @@
     for half in range(2):
         lanes = slice(128 * half, 128 * half + 128)
         if half == 1:
+            reads[8].wait()
             reads[9].wait()
-            reads[10].wait()
 
         def step(x, carry, half=half, lanes=lanes):
             rows = pl.ds(pl.multiple_of(x * 64, 64), 64)
             hidden = spec_ref[rows, lanes] + hidden_ref[rows, lanes]
             normed = (hidden - mean) * scale + bias
             level = jnp.concatenate(
-                [index_ref[half, pl.ds(z * 16 + x, 16, stride=64), :] for z in range(4)], axis=0
+                [index_ref[half, pl.ds(z * 16 + x, 16, stride=PITCH), :] for z in range(4)], axis=0
             ).astype(F32)
             local = jnp.clip(normed * 1.25 + (2.5 - level), 0.0, 1.0)
             other = 1.0 - local
@@ -481,18 +474,20 @@
             product = dot(weights, jnp.concatenate(columns, axis=1))
             for z in range(4):
                 value = product[0:16, 128 * z : 128 * z + 128] + product[16:32, 128 * z : 128 * z + 128]
-                result_ref[half, pl.ds(z * 16 + x, 16, stride=64), :] = value + constant
+                result_ref[half, pl.ds(z * 16 + x, 16, stride=PITCH), :] = value + constant
             return carry
 
         for part in range(2):
             lax.fori_loop(8 * part, 8 * part + 8, step, 0, unroll=8)
-            copy = pltpu.make_async_copy(
-                result_ref.at[half].reshape(64, 16, 128).at[:, 8 * part : 8 * part + 8, :],
-                out_ref.at[:, 8 * part : 8 * part + 8, lanes],
-                sems.at[2 * half + part],
-            )
-            copy.start()
-            copies.append(copy)
+            for z in range(4):
+                row = 16 * z + 8 * part
+                copy = pltpu.make_async_copy(
+                    result_ref.at[half].reshape(16, PITCH, 128).at[:, row : row + 8, :],
+                    out_ref.at[:, row : row + 8, lanes],
+                    sems.at[8 * half + 4 * part + z],
+                )
+                copy.start()
+                copies.append(copy)
     for copy in copies:
         copy.wait()
 
@@ -519,6 +514,14 @@
 
 def shape(dims, dtype=F32):
     return jax.ShapeDtypeStruct(dims, dtype)
+
+
+def far(*arrays):
+    return [pltpu.with_memory_space_constraint(array, pltpu.HBM) for array in arrays]
+
+
+def near(*arrays):
+    return [pltpu.with_memory_space_constraint(array, pltpu.VMEM) for array in arrays]
 
 
 def transfers(count):
@@ -529,7 +532,7 @@
     y_high, y_low = split_table(Y_FORWARD)
     return pl.pallas_call(
         forward_kernel,
-        out_shape=(shape((512, 128)), shape((128, 128)), shape((128, 128))),
+        out_shape=(pltpu.VMEM((512, 128), F32), pltpu.VMEM((128, 128), F32), pltpu.VMEM((128, 128), F32)),
         in_specs=[hbm()] * 4,
         out_specs=(whole(),) * 3,
         scratch_shapes=[
@@ -541,61 +544,61 @@
             pltpu.VMEM((4, 256, 256), B16),
             transfers(5),
         ],
-        compiler_params=params(60),
+        compiler_params=params(24),
         cost_estimate=cost(4 * 10**8, 4 * 10**6),
         name="forward",
     )(
-        jnp.asarray(PHASE), field, weight,
-        jnp.asarray(np.concatenate([y_high, y_low], axis=2)),
+        *far(jnp.asarray(PHASE), field, weight, jnp.asarray(np.concatenate([y_high, y_low], axis=2)))
     )
 
 
 def local_call(field, local_weight, base_weight, spline_coef):
     return pl.pallas_call(
         local_kernel,
-        out_shape=(shape((1024, 256)), shape((32, 128)), shape((32, 256), B16), shape((16, 128))),
-        in_specs=[hbm()] + [whole()] * 3,
-        out_specs=(hbm(),) * 4,
+        out_shape=(
+            pltpu.HBM((1024, 256), F32), pltpu.VMEM((32, 128), F32), pltpu.HBM((32, 256), B16), pltpu.HBM((16, 128), F32),
+        ),
+        in_specs=[hbm()] * 4,
+        out_specs=(hbm(), whole(), hbm(), hbm()),
         scratch_shapes=[
-            pltpu.VMEM((2, 1024, 128), F32),
+            pltpu.VMEM((16, 16), F32),
+            pltpu.VMEM((16, 16), F32),
+            pltpu.VMEM((16, 8, 16), F32),
+            pltpu.VMEM((2, 16 * PITCH, 128), F32),
             pltpu.VMEM((1024, 256), F32),
-            pltpu.VMEM((32, 128), F32),
             pltpu.VMEM((32, 256), B16),
             pltpu.VMEM((16, 128), F32),
-            transfers(2),
-            transfers(4),
+            transfers(5),
+            transfers(3),
         ],
-        compiler_params=params(60),
+        compiler_params=params(24),
         cost_estimate=cost(10**8, 2 * 10**6),
         name="local",
-    )(field, local_weight, base_weight, jnp.transpose(spline_coef, (0, 2, 1)))
+    )(*far(field.reshape(16, 64, 256), local_weight, base_weight, jnp.transpose(spline_coef, (0, 2, 1))))
 
 
 def mix_call(got, weight, partner, kept, local_weight, stat):
     return pl.pallas_call(
         mix_kernel,
-        out_shape=shape((768, 128)),
-        in_specs=[hbm()] * 9,
+        out_shape=pltpu.VMEM((768, 128), F32),
+        in_specs=[whole()] * 4 + [hbm()] * 5,
         out_specs=whole(),
         scratch_shapes=[
             pltpu.SMEM((2, 512), F32),
-            pltpu.VMEM((512, 128), F32),
             pltpu.VMEM((16, 16), F32),
             pltpu.VMEM((256, 128), F32),
             pltpu.VMEM((128, 64), F32),
             pltpu.VMEM((128, 128), F32),
             pltpu.VMEM((1024, 32), F32),
-            pltpu.VMEM((128, 128), F32),
-            pltpu.VMEM((32, 128), F32),
             pltpu.VMEM((256, 128), F32),
-            transfers(8),
+            transfers(5),
         ],
-        compiler_params=params(60),
+        compiler_params=params(24),
         cost_estimate=cost(10**7, 10**6),
         name="mix",
     )(
-        jnp.asarray(PHASE), got, weight, partner, kept, local_weight, stat,
-        jnp.asarray(Z_FORWARD, F32), jnp.asarray(Z_BACK, F32),
+        *near(got, partner, kept, stat),
+        *far(jnp.asarray(PHASE), weight, local_weight, jnp.asarray(Z_FORWARD, F32), jnp.asarray(Z_BACK, F32)),
     )
 
 
@@ -603,30 +606,32 @@
     y_high, y_low = split_table(Y_BACK)
     return pl.pallas_call(
         output_kernel,
-        out_shape=shape((64, 16, 256)),
-        in_specs=[hbm()] * 9,
+        out_shape=pltpu.HBM((16, 64, 256), F32),
+        in_specs=[whole()] + [hbm()] * 8,
         out_specs=hbm(),
         scratch_shapes=[
             pltpu.VMEM((1, 16), F32),
             pltpu.VMEM((1, 16), F32),
-            pltpu.VMEM((768, 128), F32),
             pltpu.VMEM((4, 128, 256), B16),
             pltpu.VMEM((4, 128, 256), B16),
             pltpu.VMEM((1024, 256), F32),
-            pltpu.VMEM((2, 1024, 128), F32),
+            pltpu.VMEM((2, 16 * PITCH, 128), F32),
             pltpu.VMEM((1024, 256), F32),
-            pltpu.VMEM((2, 1024, 128), jnp.int32),
+            pltpu.VMEM((2, 16 * PITCH, 128), jnp.int32),
             pltpu.VMEM((32, 256), B16),
             pltpu.VMEM((16, 128), F32),
-            transfers(11),
-            transfers(4),
+            transfers(10),
+            transfers(16),
         ],
-        compiler_params=params(60),
+        compiler_params=params(24),
         cost_estimate=cost(10**9, 6 * 10**6),
         name="output",
     )(
-        back, hidden, index, kan, constant, bn_gain.reshape(1, 16), bn_shift.reshape(1, 16),
-        jnp.asarray(y_high), jnp.asarray(y_low),
+        *near(back),
+        *far(
+            hidden, index.reshape(16, 64, 256), kan, constant, bn_gain.reshape(1, 16), bn_shift.reshape(1, 16),
+            jnp.asarray(y_high), jnp.asarray(y_low),
+        ),
     )
 
 

time: 72.1 us -> 68.4 us (0.949)
  Pallas kernels: 18.3 us -> 14.8 us
  waiting for transfers between devices: 0.42 us -> 1.44 us
    pallas_call x4, Pallas kernels: 18.3 us -> 14.8 us  [the longest x1 5.61 us: output_call(): pl.pallas_call(output_kernel, out_shape=pltpu.HBM((16, 64, 256), F32), in...]
    ppermute x1, waiting for transfers between devices: 0.01 us -> 0.73 us  [on_device(): lax.ppermute(own, BOTH, [(16 * a, 16 * b) for a, b in zip(path[:-1], path...]
  transfers between devices with their start and end apart: 2 -> 2, of which waited for: 1 -> 2; matrix products, arithmetic and copies ran while one was open for 0% -> 0% of each run, Pallas kernels for 6% -> 5%
where the time goes in v3:
time: 68.4 us; the launch traced here: 68.1 us
  starting transfers between devices  26.4 us (39%)
  blocking collectives  25.5 us (37%)
  Pallas kernels  14.8 us (22%)
  waiting for transfers between devices  1.44 us (2%)
    all_to_all x1, blocking collectives, on_device(): lax.all_to_all(back.reshape(256, 1, 384), BOTH, 0, 0, tiled=True)  25.5 us
    all_to_all x1, starting transfers between devices, on_device(): lax.all_to_all(sent.reshape(256, 2, 128), BOTH, 0, 0, tiled=True)  15.7 us
    ppermute x1, starting transfers between devices, on_device(): lax.ppermute(own, BOTH, [(16 * a, 16 * b) for a, b in zip(path[:-1], path...  10.7 us
    pallas_call x1, Pallas kernels, output_call(): pl.pallas_call(output_kernel, out_shape=pltpu.HBM((16, 64, 256), F32), in...  5.61 us
    pallas_call x1, Pallas kernels, local_call(): pl.pallas_call(local_kernel, out_shape=(pltpu.HBM((1024, 256), F32), pltp...  3.26 us
    pallas_call x1, Pallas kernels, forward_call(): pl.pallas_call(forward_kernel, out_shape=(pltpu.VMEM((512, 128), F32), pl...  3.14 us
    pallas_call x1, Pallas kernels, mix_call(): pl.pallas_call(mix_kernel, out_shape=pltpu.VMEM((768, 128), F32), in_spec...  2.77 us
  transfers between devices with their start and end apart: 2, of which 2 were waited for; matrix products, arithmetic and copies ran while one was open for 0% of the time, Pallas kernels for 5%

profile of v3, /device:TPU:1, one launch (start us, length us, event | category | flops | bytes accessed | tf_op | source)
XLA Modules:
  0.0 68.1 jit_solution(5893245158759809347)
XLA Ops:
  0.0 3.1 %forward.1 = (f32[512,128]{1,0:T(8,128)}, f32[128,128]{1,0:T(8,128)S(1)}, f32[128,128]{1,0:T(8,128)S(1)}) custom-call(f32[2,512]{1,0:T(2,128)} %constant.12.clone.phase_hbm, f32[1024,256]{1,0:T(8,128)} %bitcast.17, f32[1024,32]{1,0:T(8,128)} %bitcast.19, bf16[4,256,256]{2,1,0:T(8,128)(2,1)} %constant.13.clone.y_hbm), custom_call_target="tpu_custom_call" | custom-call | flops 400000000 | bytes 4000000 | tf_op jit(solution)/shard_map/forward/pallas_call | solution.py:533
  3.1 15.7 %all-to-all-start = ((f32[256,2,128]{2,1,0:T(2,128)}), f32[256,2,128]{2,1,0:T(2,128)S(1)}, u32[]{:S(2)}, u32[]{:S(2)}) async-start(f32[256,2,128]{2,1,0:T(2,128)} %bitcast.3), calls=%async_computation | async-start | bytes 524288 | tf_op jit(solution)/shard_map/all_to_all | solution.py:649
  18.8 10.7 %collective-permute-start = (f32[128,128]{1,0:T(8,128)S(1)}, f32[128,128]{1,0:T(8,128)S(1)}, u32[]{:S(2)}, u32[]{:S(2)}) collective-permute-start(f32[128,128]{1,0:T(8,128)S(1)} %get-tuple-element.13), channel_id=1, source_target_pairs={{0,240},{240,16},{16,224},{224,32},{32,208},{208,48},{48,192},{192... | collective-permute-start | bytes 196616 | tf_op jit(solution)/shard_map/ppermute | solution.py:648
  29.5 3.3 %local.1 = (f32[1024,256]{1,0:T(8,128)}, f32[32,128]{1,0:T(8,128)S(1)}, bf16[32,256]{1,0:T(8,128)(2,1)}, f32[16,128]{1,0:T(8,128)}) custom-call(f32[16,64,256]{2,1,0:T(8,128)} %bitcast.18, f32[16,16]{1,0:T(8,128)} %map_hbm.3, f32[16,16]{1,0:T(8,128)} %base_hbm.1, f32[16,8,16]{2,1,0:T(8,128)} %bitcast.22), custom_call_target="tpu_custom_call" | custom-call | flops 100000000 | bytes 2000000 | tf_op jit(solution)/shard_map/local/pallas_call | solution.py:556
  32.8 0.7 %collective-permute-done.partner_ref = f32[128,128]{1,0:T(8,128)S(1)} collective-permute-done((f32[128,128]{1,0:T(8,128)S(1)}, f32[128,128]{1,0:T(8,128)S(1)}, u32[]{:S(2)}, u32[]{:S(2)}) %collective-permute-start) | collective-permute-done | bytes 65568 | tf_op jit(solution)/shard_map/ppermute | solution.py:648
  33.5 0.7 %all-to-all-done = f32[256,2,128]{2,1,0:T(2,128)S(1)} async-done(((f32[256,2,128]{2,1,0:T(2,128)}), f32[256,2,128]{2,1,0:T(2,128)S(1)}, u32[]{:S(2)}, u32[]{:S(2)}) %all-to-all-start) | async-done | bytes 262176 | tf_op jit(solution)/shard_map/all_to_all | solution.py:649
  34.2 2.8 %mix.1 = f32[768,128]{1,0:T(8,128)S(1)} custom-call(f32[512,128]{1,0:T(8,128)S(1)} %bitcast.16, f32[128,128]{1,0:T(8,128)S(1)} %collective-permute-done.partner_ref, f32[128,128]{1,0:T(8,128)S(1)} %get-tuple-element.14.kept_ref, f32[32,128]{1,0:T(8,128)S(1)} %get-tuple-element.15.stat_ref, f32[2,512]{1,0:T(2,128)} %constant.12.clone.phase_hbm, ...), custom_call_target="tpu_custom_call" | custom-call | flops 10000000 | bytes 1000000 | tf_op jit(solution)/shard_map/mix/pallas_call | solution.py:581
  37.0 25.5 %all_to_all.10 = f32[256,1,384]{2,1,0:T(1,128)S(1)} all-to-all(f32[256,1,384]{2,1,0:T(1,128)S(1)} %bitcast.15), channel_id=1, replica_groups=mesh['pa'=16,'pb'=16] {'pa','pb'}, dimensions={0} | all-to-all | bytes 786432 | tf_op jit(solution)/shard_map/all_to_all | solution.py:652
  62.5 5.6 %output.1 = f32[16,64,256]{2,1,0:T(8,128)} custom-call(f32[768,128]{1,0:T(8,128)S(1)} %bitcast.14, f32[1024,256]{1,0:T(8,128)} %get-tuple-element.16.hidden_hbm, s32[16,64,256]{2,1,0:T(8,128)} %bitcast.21, bf16[32,256]{1,0:T(8,128)(2,1)} %get-tuple-element.17.kan_hbm, f32[16,128]{1,0:T(8,128)} %get-tuple-element.18.constant_hbm, f32[1,16]{1,0:T(1,128)} %bitcast.23, ...), custom_call_target="tpu_custom_call" | custom-call | flops 1000000000 | bytes 6000000 | tf_op jit(solution)/shard_map/output/pallas_call | solution.py:607
Async XLA Ops:
  3.1 31.1 %all-to-all-start = ((f32[256,2,128]{2,1,0:T(2,128)}), f32[256,2,128]{2,1,0:T(2,128)S(1)}, u32[]{:S(2)}, u32[]{:S(2)}) async-start(f32[256,2,128]{2,1,0:T(2,128)} %bitcast.3), calls=%async_computation | async-start | bytes 524288 | tf_op jit(solution)/shard_map/all_to_all | solution.py:649
  18.8 14.7 %collective-permute-start = (f32[128,128]{1,0:T(8,128)S(1)}, f32[128,128]{1,0:T(8,128)S(1)}, u32[]{:S(2)}, u32[]{:S(2)}) collective-permute-start(f32[128,128]{1,0:T(8,128)S(1)} %get-tuple-element.13), channel_id=1, source_target_pairs={{0,240},{240,16},{16,224},{224,32},{32,208},{208,48},{48,192},{192... | collective-permute-start | bytes 196616 | tf_op jit(solution)/shard_map/ppermute | solution.py:648

commit v4 on v3

--- a/solution.py
+++ b/solution.py
@@ -34,12 +34,11 @@
 
 
 def tables():
-    same_x = np.eye(4)
     angle = 2 * np.pi * (np.arange(NY)[:, None] * KY % NY) / NY
     y_part = np.stack([np.cos(angle), -np.sin(angle)], axis=1)
-    y_forward = np.einsum("jJ,ypk->jyJpk", same_x, y_part).reshape(4, NY, 128)
+    y_forward = np.tile(y_part.reshape(NY, 32), (1, 4))
     weight = np.where(KY == 0, 1.0, 2.0) / CELLS
-    y_back = np.einsum("jJ,ypk,k->jpJky", same_x, y_part, weight).reshape(4, 128, NY)
+    y_back = np.einsum("ypk,k->pky", y_part, weight).reshape(32, NY)
     z = 4 * np.arange(16)[None, :] + np.arange(4)[:, None]
     angle = 2 * np.pi * (z[:, :, None] * KZ % NZ) / NZ
     z_forward = np.einsum("qpzaj,hH->pzhaqHj", rotation(angle, -1.0), np.eye(2)).reshape(256, 128)
@@ -95,16 +94,16 @@
 
 def forward_kernel(
     phase_hbm, field_hbm, weight_hbm, y_hbm, out_ref, sent_ref, kept_ref,
-    phase_ref, half_ref, rows_ref, field_ref, weight_ref, y_ref, sems,
+    phase_ref, half_ref, rows_ref, field_ref, weight_ref, small_ref, y_ref, sems,
 ):
     pa, pb = lax.axis_index("pa"), lax.axis_index("pb")
     copies = [
         pltpu.make_async_copy(source, target, sems.at[number])
         for number, (source, target) in enumerate(
             [
+                (y_hbm, small_ref),
                 (field_hbm.at[:, 0:128], field_ref.at[0]),
                 (field_hbm.at[:, 128:256], field_ref.at[1]),
-                (y_hbm, y_ref),
                 (weight_hbm, weight_ref),
                 (phase_hbm, phase_ref),
             ]
@@ -112,7 +111,12 @@
     ]
     for copy in copies:
         copy.start()
-    for copy in copies[0:3]:
+    copies[0].wait()
+    small = small_ref[...].reshape(16, 16, 256)
+    for xj in range(4):
+        mine = (iota((16, 256), 1) % 128 // 32 == xj).astype(F32).astype(B16)
+        y_ref[xj] = (small * mine[None]).reshape(256, 256)
+    for copy in copies[1:3]:
         copy.wait()
     total = jnp.zeros((256, 128), F32)
     for xj in range(4):
@@ -156,8 +160,9 @@
 
 
 def local_kernel(
-    field_hbm, map_hbm, base_hbm, coef_hbm, hidden_hbm, stat_ref, kan_hbm, shift_hbm,
-    map_ref, base_ref, coef_ref, field_ref, hidden_ref, kan_ref, shift_ref, sems, out_sems,
+    field_hbm, map_hbm, base_hbm, coef_hbm, index_hbm, y_hbm, gain_hbm, bias_hbm,
+    hidden_ref, stat_ref, kan_ref, shift_ref, index_ref, y_ref, gain_ref, bias_ref,
+    map_ref, base_ref, coef_ref, field_ref, row_ref, sems,
 ):
     copies = [
         pltpu.make_async_copy(
@@ -170,8 +175,19 @@
     small = [
         pltpu.make_async_copy(source, target, sems.at[2 + number])
         for number, (source, target) in enumerate([(map_hbm, map_ref), (base_hbm, base_ref), (coef_hbm, coef_ref)])
+    ] + [
+        pltpu.make_async_copy(gain_hbm, row_ref.at[0:1, :], sems.at[8]),
+        pltpu.make_async_copy(bias_hbm, row_ref.at[1:2, :], sems.at[9]),
     ]
-    for copy in small + copies:
+    moved = [pltpu.make_async_copy(y_hbm, y_ref, sems.at[7])] + [
+        pltpu.make_async_copy(
+            index_hbm.at[:, :, 128 * half : 128 * half + 128],
+            index_ref.at[half].reshape(16, PITCH, 128).at[:, 0:64, :],
+            sems.at[5 + half],
+        )
+        for half in range(2)
+    ]
+    for copy in small + copies + moved:
         copy.start()
     for copy in small:
         copy.wait()
@@ -183,14 +199,8 @@
     kan_ref[16:32, 0:128] = low
     kan_ref[16:32, 128:256] = jnp.zeros((16, 128), B16)
     shift_ref[...] = jnp.broadcast_to(jnp.sum(last, axis=1, keepdims=True), (16, 128))
-    outs = [
-        pltpu.make_async_copy(source, target, out_sems.at[number])
-        for number, (source, target) in enumerate(
-            [(kan_ref, kan_hbm), (shift_ref, shift_hbm), (hidden_ref, hidden_hbm)]
-        )
-    ]
-    outs[0].start()
-    outs[1].start()
+    gain_ref[...] = jnp.broadcast_to(column(row_ref[0:1, :]), (16, 128))
+    bias_ref[...] = jnp.broadcast_to(column(row_ref[1:2, :]), (16, 128))
     high, low = split(map_ref[...])
     zero = jnp.zeros((16, 16), B16)
     maps = jnp.concatenate(
@@ -211,7 +221,6 @@
         return total
 
     total = lax.fori_loop(0, 16, step, jnp.zeros((16, 256), F32), unroll=4)
-    outs[2].start()
     mean = jnp.sum(total, axis=1, keepdims=True) * (1.0 / BLOCK_CELLS)
 
     def spread(part, total):
@@ -226,7 +235,7 @@
     first = iota((16, 128), 1) == 0
     stat_ref[0:16, :] = jnp.where(first, mean, 0.0)
     stat_ref[16:32, :] = jnp.where(first, squares, 0.0)
-    for copy in outs:
+    for copy in moved:
         copy.wait()
 
 
@@ -348,30 +357,9 @@
 
 
 def output_kernel(
-    got_ref, hidden_hbm, index_hbm, kan_hbm, constant_hbm, gain_hbm, bias_hbm,
-    y_high_hbm, y_low_hbm, out_ref,
-    gain_ref, bias_ref, y_high_ref, y_low_ref,
-    spec_ref, result_ref, hidden_ref, index_ref, kan_ref, constant_ref, in_sems, sems,
+    got_ref, hidden_ref, kan_ref, constant_ref, index_ref, small_ref, gain_ref, bias_ref, out_ref,
+    y_high_ref, y_low_ref, spec_ref, result_ref, sems,
 ):
-    reads = [
-        pltpu.make_async_copy(source, target, in_sems.at[number])
-        for number, (source, target) in enumerate(
-            [
-                (gain_hbm, gain_ref),
-                (bias_hbm, bias_ref),
-                (y_high_hbm, y_high_ref),
-                (y_low_hbm, y_low_ref),
-                (kan_hbm, kan_ref),
-                (constant_hbm, constant_ref),
-                (hidden_hbm.at[:, 0:128], hidden_ref.at[:, 0:128]),
-                (index_hbm.at[:, :, 0:128], index_ref.at[0].reshape(16, PITCH, 128).at[:, 0:64, :]),
-                (hidden_hbm.at[:, 128:256], hidden_ref.at[:, 128:256]),
-                (index_hbm.at[:, :, 128:256], index_ref.at[1].reshape(16, PITCH, 128).at[:, 0:64, :]),
-            ]
-        )
-    ]
-    for copy in reads:
-        copy.start()
     stats = got_ref[pl.ds(2, 256, stride=3), :]
     sums = jnp.sum(stats, axis=0, keepdims=True)
     mean = sums * (1.0 / 256)
@@ -389,12 +377,10 @@
     pick = (owner == row).astype(F32)
     mean = dot_nt(pick, jnp.broadcast_to(mean, (8, 128)), EXACT)[:, 0:1]
     variance = dot_nt(pick, jnp.broadcast_to(variance, (8, 128)), EXACT)[:, 0:1]
-    reads[0].wait()
-    reads[1].wait()
-    scale = column(gain_ref[...]) * lax.rsqrt(variance + EPSILON)
+    scale = gain_ref[:, 0:1] * lax.rsqrt(variance + EPSILON)
     mean = jnp.broadcast_to(jnp.concatenate([mean] * 4, axis=0), (64, 128))
     scale = jnp.broadcast_to(jnp.concatenate([scale] * 4, axis=0), (64, 128))
-    bias = jnp.broadcast_to(jnp.concatenate([column(bias_ref[...])] * 4, axis=0), (64, 128))
+    bias = jnp.broadcast_to(jnp.concatenate([bias_ref[:, 0:1]] * 4, axis=0), (64, 128))
     lines = [[None] * 2 for _ in range(16)]
     sign = signs(8, -1.0)
     for half in range(2):
@@ -416,24 +402,24 @@
         groups.append(jnp.concatenate([piece[0:64], piece[64:128]], axis=1))
     high, low = split(jnp.concatenate(groups, axis=0))
     both = jnp.concatenate([high, low], axis=0)
-    reads[2].wait()
-    reads[3].wait()
+    for number, table in enumerate((y_high_ref, y_low_ref)):
+        table[...] = jnp.zeros((4, 128, 256), B16)
+        for xj in range(4):
+            for part in range(2):
+                start = 32 * number + 16 * part
+                row = 64 * part + 16 * xj
+                table[xj, row : row + 16, :] = small_ref[start : start + 16, :]
     for xj in range(4):
         product = dot(both, y_high_ref[xj])
         value = product[0:256] + product[256:512] + dot(high, y_low_ref[xj])
         for x4 in range(4):
             start = (4 * x4 + xj) * 64
             spec_ref[start : start + 64, :] = value[64 * x4 : 64 * x4 + 64]
-    for copy in reads[4:8]:
-        copy.wait()
     weights = kan_ref[...]
     constant = constant_ref[...]
     copies = []
     for half in range(2):
         lanes = slice(128 * half, 128 * half + 128)
-        if half == 1:
-            reads[8].wait()
-            reads[9].wait()
 
         def step(x, carry, half=half, lanes=lanes):
             rows = pl.ds(pl.multiple_of(x * 64, 64), 64)
@@ -541,6 +527,7 @@
             pltpu.VMEM((1024, 128), F32),
             pltpu.VMEM((2, 1024, 128), F32),
             pltpu.VMEM((1024, 32), F32),
+            pltpu.VMEM((256, 256), B16),
             pltpu.VMEM((4, 256, 256), B16),
             transfers(5),
         ],
@@ -548,33 +535,36 @@
         cost_estimate=cost(4 * 10**8, 4 * 10**6),
         name="forward",
     )(
-        *far(jnp.asarray(PHASE), field, weight, jnp.asarray(np.concatenate([y_high, y_low], axis=2)))
-    )
-
-
-def local_call(field, local_weight, base_weight, spline_coef):
+        *far(jnp.asarray(PHASE), field, weight, jnp.asarray(np.concatenate([y_high, y_low], axis=1)))
+    )
+
+
+def local_call(field, local_weight, base_weight, spline_coef, index, bn_gain, bn_shift):
+    y_table = np.concatenate(split_table(Y_BACK), axis=0)
     return pl.pallas_call(
         local_kernel,
         out_shape=(
-            pltpu.HBM((1024, 256), F32), pltpu.VMEM((32, 128), F32), pltpu.HBM((32, 256), B16), pltpu.HBM((16, 128), F32),
+            pltpu.VMEM((1024, 256), F32), pltpu.VMEM((32, 128), F32), pltpu.VMEM((32, 256), B16), pltpu.VMEM((16, 128), F32),
+            pltpu.VMEM((2, 16 * PITCH, 128), jnp.int32),
+            pltpu.VMEM((64, 256), B16),
+            pltpu.VMEM((16, 128), F32),
+            pltpu.VMEM((16, 128), F32),
         ),
-        in_specs=[hbm()] * 4,
-        out_specs=(hbm(), whole(), hbm(), hbm()),
+        in_specs=[hbm()] * 8,
+        out_specs=(whole(),) * 8,
         scratch_shapes=[
             pltpu.VMEM((16, 16), F32),
             pltpu.VMEM((16, 16), F32),
             pltpu.VMEM((16, 8, 16), F32),
             pltpu.VMEM((2, 16 * PITCH, 128), F32),
-            pltpu.VMEM((1024, 256), F32),
-            pltpu.VMEM((32, 256), B16),
-            pltpu.VMEM((16, 128), F32),
-            transfers(5),
-            transfers(3),
+            pltpu.VMEM((2, 16), F32),
+            transfers(10),
         ],
         compiler_params=params(24),
         cost_estimate=cost(10**8, 2 * 10**6),
         name="local",
-    )(*far(field.reshape(16, 64, 256), local_weight, base_weight, jnp.transpose(spline_coef, (0, 2, 1))))
+    )(*far(field.reshape(16, 64, 256), local_weight, base_weight, jnp.transpose(spline_coef, (0, 2, 1)), index.reshape(16, 64, 256),
+            jnp.asarray(y_table), bn_gain.reshape(1, 16), bn_shift.reshape(1, 16)))
 
 
 def mix_call(got, weight, partner, kept, local_weight, stat):
@@ -602,37 +592,23 @@
     )
 
 
-def output_call(back, hidden, index, kan, constant, bn_gain, bn_shift):
-    y_high, y_low = split_table(Y_BACK)
+def output_call(back, hidden, kan, constant, index, y_table, gain, bias):
     return pl.pallas_call(
         output_kernel,
         out_shape=pltpu.HBM((16, 64, 256), F32),
-        in_specs=[whole()] + [hbm()] * 8,
+        in_specs=[whole()] * 8,
         out_specs=hbm(),
         scratch_shapes=[
-            pltpu.VMEM((1, 16), F32),
-            pltpu.VMEM((1, 16), F32),
             pltpu.VMEM((4, 128, 256), B16),
             pltpu.VMEM((4, 128, 256), B16),
             pltpu.VMEM((1024, 256), F32),
             pltpu.VMEM((2, 16 * PITCH, 128), F32),
-            pltpu.VMEM((1024, 256), F32),
-            pltpu.VMEM((2, 16 * PITCH, 128), jnp.int32),
-            pltpu.VMEM((32, 256), B16),
-            pltpu.VMEM((16, 128), F32),
-            transfers(10),
             transfers(16),
         ],
         compiler_params=params(24),
         cost_estimate=cost(10**9, 6 * 10**6),
         name="output",
-    )(
-        *near(back),
-        *far(
-            hidden, index.reshape(16, 64, 256), kan, constant, bn_gain.reshape(1, 16), bn_shift.reshape(1, 16),
-            jnp.asarray(y_high), jnp.asarray(y_low),
-        ),
-    )
+    )(*near(back, hidden, kan, constant, index, y_table, gain, bias))
 
 
 def on_device(
@@ -647,10 +623,12 @@
         path.append(15 - path[-1] if path[-1] < 8 else 16 - path[-1])
     partner = lax.ppermute(own, BOTH, [(16 * a, 16 * b) for a, b in zip(path[:-1], path[1:])])
     got = lax.all_to_all(sent.reshape(256, 2, 128), BOTH, 0, 0, tiled=True).reshape(512, 128)
-    hidden, stat, kan, constant = local_call(field, local_weight, base_weight, spline_coef)
+    hidden, stat, *rest = local_call(
+        field, local_weight, base_weight, spline_coef, index, bn_gain, bn_shift
+    )
     back = mix_call(got, weight, partner, kept, local_weight, stat)
     back = lax.all_to_all(back.reshape(256, 1, 384), BOTH, 0, 0, tiled=True).reshape(768, 128)
-    output = output_call(back, hidden, index, kan, constant, bn_gain, bn_shift)
+    output = output_call(back, hidden, *rest)
     return output.reshape(16, 4, 16, 256)
 
 

time: 68.4 us -> 66.8 us (0.977)
  Pallas kernels: 14.8 us -> 12.6 us
    pallas_call x1, Pallas kernels: 5.61 us -> 4.17 us  [output_call(): pl.pallas_call(output_kernel, out_shape=pltpu.HBM((16, 64, 256), F32), in...]
  transfers between devices with their start and end apart: 2 -> 2, of which waited for: 2 -> 2; matrix products, arithmetic and copies ran while one was open for 0% -> 0% of each run, Pallas kernels for 5% -> 4%
where the time goes in v4:
time: 66.8 us; the launch traced here: 66.6 us
  starting transfers between devices  26.4 us (40%)
  blocking collectives  25.5 us (38%)
  Pallas kernels  12.6 us (19%)
  waiting for transfers between devices  2.07 us (3%)
    all_to_all x1, blocking collectives, on_device(): lax.all_to_all(back.reshape(256, 1, 384), BOTH, 0, 0, tiled=True)  25.5 us
    all_to_all x1, starting transfers between devices, on_device(): lax.all_to_all(sent.reshape(256, 2, 128), BOTH, 0, 0, tiled=True)  15.7 us
    ppermute x1, starting transfers between devices, on_device(): lax.ppermute(own, BOTH, [(16 * a, 16 * b) for a, b in zip(path[:-1], path...  10.7 us
    pallas_call x1, Pallas kernels, output_call(): pl.pallas_call(output_kernel, out_shape=pltpu.HBM((16, 64, 256), F32), in...  4.17 us
    pallas_call x1, Pallas kernels, forward_call(): pl.pallas_call(forward_kernel, out_shape=(pltpu.VMEM((512, 128), F32), pl...  3.05 us
    pallas_call x1, Pallas kernels, mix_call(): pl.pallas_call(mix_kernel, out_shape=pltpu.VMEM((768, 128), F32), in_spec...  2.77 us
    pallas_call x1, Pallas kernels, local_call(): pl.pallas_call(local_kernel, out_shape=(pltpu.VMEM((1024, 256), F32), plt...  2.62 us
    ppermute x1, waiting for transfers between devices, on_device(): lax.ppermute(own, BOTH, [(16 * a, 16 * b) for a, b in zip(path[:-1], path...  1.37 us
  transfers between devices with their start and end apart: 2, of which 2 were waited for; matrix products, arithmetic and copies ran while one was open for 0% of the time, Pallas kernels for 4%

profile of v4, /device:TPU:1, one launch (start us, length us, event | category | flops | bytes accessed | tf_op | source)
XLA Modules:
  0.0 66.6 jit_solution(1658726821092793210)
XLA Ops:
  0.0 3.1 %forward.1 = (f32[512,128]{1,0:T(8,128)}, f32[128,128]{1,0:T(8,128)S(1)}, f32[128,128]{1,0:T(8,128)S(1)}) custom-call(f32[2,512]{1,0:T(2,128)} %constant.10.clone.phase_hbm, f32[1024,256]{1,0:T(8,128)} %bitcast.17, f32[1024,32]{1,0:T(8,128)} %bitcast.19, bf16[256,256]{1,0:T(8,128)(2,1)} %constant.11.clone.y_hbm), custom_call_target="tpu_custom_call" | custom-call | flops 400000000 | bytes 4000000 | tf_op jit(solution)/shard_map/forward/pallas_call | solution.py:519
  3.1 15.7 %all-to-all-start = ((f32[256,2,128]{2,1,0:T(2,128)}), f32[256,2,128]{2,1,0:T(2,128)S(1)}, u32[]{:S(2)}, u32[]{:S(2)}) async-start(f32[256,2,128]{2,1,0:T(2,128)} %bitcast.3), calls=%async_computation | async-start | bytes 524288 | tf_op jit(solution)/shard_map/all_to_all | solution.py:625
  18.7 10.7 %collective-permute-start = (f32[128,128]{1,0:T(8,128)S(1)}, f32[128,128]{1,0:T(8,128)S(1)}, u32[]{:S(2)}, u32[]{:S(2)}) collective-permute-start(f32[128,128]{1,0:T(8,128)S(1)} %get-tuple-element.17), channel_id=1, source_target_pairs={{0,240},{240,16},{16,224},{224,32},{32,208},{208,48},{48,192},{192... | collective-permute-start | bytes 196616 | tf_op jit(solution)/shard_map/ppermute | solution.py:624
  29.4 2.6 %local.1 = (f32[1024,256]{1,0:T(8,128)S(1)}, f32[32,128]{1,0:T(8,128)S(1)}, bf16[32,256]{1,0:T(8,128)(2,1)S(1)}, f32[16,128]{1,0:T(8,128)S(1)}, s32[2,1152,128]{...) custom-call(f32[16,64,256]{2,1,0:T(8,128)} %bitcast.18, ...), custom_call_target="tpu_custom_call" | custom-call | flops 100000000 | bytes 2000000 | tf_op jit(solution)/shard_map/local/pallas_call | solution.py:544
  32.1 1.4 %collective-permute-done.partner_ref = f32[128,128]{1,0:T(8,128)S(1)} collective-permute-done((f32[128,128]{1,0:T(8,128)S(1)}, f32[128,128]{1,0:T(8,128)S(1)}, u32[]{:S(2)}, u32[]{:S(2)}) %collective-permute-start) | collective-permute-done | bytes 65568 | tf_op jit(solution)/shard_map/ppermute | solution.py:624
  33.4 0.7 %all-to-all-done = f32[256,2,128]{2,1,0:T(2,128)S(1)} async-done(((f32[256,2,128]{2,1,0:T(2,128)}), f32[256,2,128]{2,1,0:T(2,128)S(1)}, u32[]{:S(2)}, u32[]{:S(2)}) %all-to-all-start) | async-done | bytes 262176 | tf_op jit(solution)/shard_map/all_to_all | solution.py:625
  34.1 2.8 %mix.1 = f32[768,128]{1,0:T(8,128)S(1)} custom-call(f32[512,128]{1,0:T(8,128)S(1)} %bitcast.16, f32[128,128]{1,0:T(8,128)S(1)} %collective-permute-done.partner_ref, f32[128,128]{1,0:T(8,128)S(1)} %get-tuple-element.18.kept_ref, f32[32,128]{1,0:T(8,128)S(1)} %get-tuple-element.19.stat_ref, f32[2,512]{1,0:T(2,128)} %constant.10.clone.phase_hbm, ...), custom_call_target="tpu_custom_call" | custom-call | flops 10000000 | bytes 1000000 | tf_op jit(solution)/shard_map/mix/pallas_call | solution.py:571
  36.9 25.5 %all_to_all.10 = f32[256,1,384]{2,1,0:T(1,128)S(1)} all-to-all(f32[256,1,384]{2,1,0:T(1,128)S(1)} %bitcast.15), channel_id=1, replica_groups=mesh['pa'=16,'pb'=16] {'pa','pb'}, dimensions={0} | all-to-all | bytes 786432 | tf_op jit(solution)/shard_map/all_to_all | solution.py:630
  62.4 4.2 %output.1 = f32[16,64,256]{2,1,0:T(8,128)} custom-call(f32[768,128]{1,0:T(8,128)S(1)} %bitcast.14, f32[1024,256]{1,0:T(8,128)S(1)} %get-tuple-element.20.hidden_ref, bf16[32,256]{1,0:T(8,128)(2,1)S(1)} %get-tuple-element.21.kan_ref, f32[16,128]{1,0:T(8,128)S(1)} %get-tuple-element.22.constant_ref, s32[2,1152,128]{2,1,0:T(8,128)S(1)} %get-tuple-element.23.index_ref, ...), custom_call_target="tpu_custom_call" | custom-call | flops 1000000000 | bytes 6000000 | tf_op jit(solution)/shard_map/output/pallas_call | solution.py:596
Async XLA Ops:
  3.1 31.1 %all-to-all-start = ((f32[256,2,128]{2,1,0:T(2,128)}), f32[256,2,128]{2,1,0:T(2,128)S(1)}, u32[]{:S(2)}, u32[]{:S(2)}) async-start(f32[256,2,128]{2,1,0:T(2,128)} %bitcast.3), calls=%async_computation | async-start | bytes 524288 | tf_op jit(solution)/shard_map/all_to_all | solution.py:625
  18.7 14.7 %collective-permute-start = (f32[128,128]{1,0:T(8,128)S(1)}, f32[128,128]{1,0:T(8,128)S(1)}, u32[]{:S(2)}, u32[]{:S(2)}) collective-permute-start(f32[128,128]{1,0:T(8,128)S(1)} %get-tuple-element.17), channel_id=1, source_target_pairs={{0,240},{240,16},{16,224},{224,32},{32,208},{208,48},{48,192},{192... | collective-permute-start | bytes 196616 | tf_op jit(solution)/shard_map/ppermute | solution.py:624

commit v5 on v4

--- a/solution.py
+++ b/solution.py
@@ -160,9 +160,9 @@
 
 
 def local_kernel(
-    field_hbm, map_hbm, base_hbm, coef_hbm, index_hbm, y_hbm, gain_hbm, bias_hbm,
-    hidden_ref, stat_ref, kan_ref, shift_ref, index_ref, y_ref, gain_ref, bias_ref,
-    map_ref, base_ref, coef_ref, field_ref, row_ref, sems,
+    field_hbm, map_hbm, base_hbm, coef_hbm, index_hbm, y_hbm, gain_hbm, bias_hbm, z_hbm, back_hbm,
+    z_ref, back_ref, map_ref, hidden_ref, stat_ref, kan_ref, shift_ref, index_ref, y_ref, gain_ref, bias_ref,
+    base_ref, coef_ref, field_ref, row_ref, sems,
 ):
     copies = [
         pltpu.make_async_copy(
@@ -179,7 +179,11 @@
         pltpu.make_async_copy(gain_hbm, row_ref.at[0:1, :], sems.at[8]),
         pltpu.make_async_copy(bias_hbm, row_ref.at[1:2, :], sems.at[9]),
     ]
-    moved = [pltpu.make_async_copy(y_hbm, y_ref, sems.at[7])] + [
+    moved = [
+        pltpu.make_async_copy(y_hbm, y_ref, sems.at[7]),
+        pltpu.make_async_copy(z_hbm, z_ref, sems.at[10]),
+        pltpu.make_async_copy(back_hbm, back_ref, sems.at[11]),
+    ] + [
         pltpu.make_async_copy(
             index_hbm.at[:, :, 128 * half : 128 * half + 128],
             index_ref.at[half].reshape(16, PITCH, 128).at[:, 0:64, :],
@@ -240,18 +244,15 @@
 
 
 def mix_kernel(
-    got_ref, partner_ref, kept_ref, stat_ref, phase_hbm, weight_hbm, map_hbm, z_hbm, back_hbm, out_ref,
-    phase_ref, map_ref, z_ref, back_ref, rows_ref, weight_ref, both_ref, sems,
+    got_ref, partner_ref, kept_ref, z_ref, back_ref, map_ref, stat_ref, phase_hbm, weight_hbm, out_ref,
+    phase_ref, rows_ref, weight_ref, both_ref, sems,
 ):
     pa, pb = lax.axis_index("pa"), lax.axis_index("pb")
     copies = [
         pltpu.make_async_copy(source, target, sems.at[number])
         for number, (source, target) in enumerate(
             [
-                (z_hbm, z_ref),
-                (map_hbm, map_ref),
                 (weight_hbm, weight_ref),
-                (back_hbm, back_ref),
                 (phase_hbm, phase_ref),
             ]
         )
@@ -265,8 +266,6 @@
     lines = jnp.concatenate([rows_ref[pl.ds(0, 16, stride=8), :], rows_ref[pl.ds(1, 16, stride=8), :]], axis=0)
     lines = lines.T
     lines = jnp.concatenate([lines[16 * q : 16 * (q + 1)] for q in range(8)], axis=1)
-    for copy in copies:
-        copy.wait()
     modes = dot_exact(lines, z_ref[...])
     real = [modes[:, 32 * k : 32 * k + 32] for k in range(2)]
     imag = [modes[:, 64 + 32 * k : 96 + 32 * k] for k in range(2)]
@@ -282,6 +281,7 @@
     local_imag = jnp.zeros((32, 32), F32)
     partner_real = jnp.zeros((32, 32), F32)
     partner_imag = jnp.zeros((32, 32), F32)
+    copies[0].wait()
     source, target = iota((128, 128), 0), iota((128, 128), 1)
     turn = jnp.logical_and(source // 32 == target // 32, source % 32 == (32 - target % 32) % 32)
     turn = jnp.logical_and(turn, target % 32 != 16).astype(F32)
@@ -336,6 +336,7 @@
     out_ref[pl.ds(2, 256, stride=3), :] = jnp.broadcast_to(sums[0:1], (256, 128))
     order = (iota((32, 32), 1) == 2 * (iota((32, 32), 0) % 16) + iota((32, 32), 0) // 16).astype(F32)
     mixed = dot_exact(order, jnp.concatenate([mixed_real, mixed_imag], axis=1))
+    copies[1].wait()
     planes = dot_nt(back_ref[...], mixed, EXACT)
     sign = signs(16, -1.0)
     for kxl in range(2):
@@ -377,7 +378,7 @@
     pick = (owner == row).astype(F32)
     mean = dot_nt(pick, jnp.broadcast_to(mean, (8, 128)), EXACT)[:, 0:1]
     variance = dot_nt(pick, jnp.broadcast_to(variance, (8, 128)), EXACT)[:, 0:1]
-    scale = gain_ref[:, 0:1] * lax.rsqrt(variance + EPSILON)
+    scale = gain_ref[:, 0:1] * lax.rsqrt(jnp.maximum(variance, 0.0) + EPSILON)
     mean = jnp.broadcast_to(jnp.concatenate([mean] * 4, axis=0), (64, 128))
     scale = jnp.broadcast_to(jnp.concatenate([scale] * 4, axis=0), (64, 128))
     bias = jnp.broadcast_to(jnp.concatenate([bias_ref[:, 0:1]] * 4, axis=0), (64, 128))
@@ -544,52 +545,49 @@
     return pl.pallas_call(
         local_kernel,
         out_shape=(
+            pltpu.VMEM((256, 128), F32),
+            pltpu.VMEM((128, 64), F32),
+            pltpu.VMEM((16, 16), F32),
             pltpu.VMEM((1024, 256), F32), pltpu.VMEM((32, 128), F32), pltpu.VMEM((32, 256), B16), pltpu.VMEM((16, 128), F32),
             pltpu.VMEM((2, 16 * PITCH, 128), jnp.int32),
             pltpu.VMEM((64, 256), B16),
             pltpu.VMEM((16, 128), F32),
             pltpu.VMEM((16, 128), F32),
         ),
-        in_specs=[hbm()] * 8,
-        out_specs=(whole(),) * 8,
+        in_specs=[hbm()] * 10,
+        out_specs=(whole(),) * 11,
         scratch_shapes=[
-            pltpu.VMEM((16, 16), F32),
             pltpu.VMEM((16, 16), F32),
             pltpu.VMEM((16, 8, 16), F32),
             pltpu.VMEM((2, 16 * PITCH, 128), F32),
             pltpu.VMEM((2, 16), F32),
-            transfers(10),
+            transfers(12),
         ],
         compiler_params=params(24),
         cost_estimate=cost(10**8, 2 * 10**6),
         name="local",
     )(*far(field.reshape(16, 64, 256), local_weight, base_weight, jnp.transpose(spline_coef, (0, 2, 1)), index.reshape(16, 64, 256),
-            jnp.asarray(y_table), bn_gain.reshape(1, 16), bn_shift.reshape(1, 16)))
-
-
-def mix_call(got, weight, partner, kept, local_weight, stat):
+            jnp.asarray(y_table), bn_gain.reshape(1, 16), bn_shift.reshape(1, 16),
+            jnp.asarray(Z_FORWARD, F32), jnp.asarray(Z_BACK, F32)))
+
+
+def mix_call(got, partner, kept, z_forward, z_back, local_weight, stat, weight):
     return pl.pallas_call(
         mix_kernel,
         out_shape=pltpu.VMEM((768, 128), F32),
-        in_specs=[whole()] * 4 + [hbm()] * 5,
+        in_specs=[whole()] * 7 + [hbm()] * 2,
         out_specs=whole(),
         scratch_shapes=[
             pltpu.SMEM((2, 512), F32),
-            pltpu.VMEM((16, 16), F32),
-            pltpu.VMEM((256, 128), F32),
-            pltpu.VMEM((128, 64), F32),
             pltpu.VMEM((128, 128), F32),
             pltpu.VMEM((1024, 32), F32),
             pltpu.VMEM((256, 128), F32),
-            transfers(5),
+            transfers(2),
         ],
         compiler_params=params(24),
         cost_estimate=cost(10**7, 10**6),
         name="mix",
-    )(
-        *near(got, partner, kept, stat),
-        *far(jnp.asarray(PHASE), weight, local_weight, jnp.asarray(Z_FORWARD, F32), jnp.asarray(Z_BACK, F32)),
-    )
+    )(*near(got, partner, kept, z_forward, z_back, local_weight, stat), *far(jnp.asarray(PHASE), weight))
 
 
 def output_call(back, hidden, kan, constant, index, y_table, gain, bias):
@@ -623,10 +621,10 @@
         path.append(15 - path[-1] if path[-1] < 8 else 16 - path[-1])
     partner = lax.ppermute(own, BOTH, [(16 * a, 16 * b) for a, b in zip(path[:-1], path[1:])])
     got = lax.all_to_all(sent.reshape(256, 2, 128), BOTH, 0, 0, tiled=True).reshape(512, 128)
-    hidden, stat, *rest = local_call(
+    z_forward, z_back, maps, hidden, stat, *rest = local_call(
         field, local_weight, base_weight, spline_coef, index, bn_gain, bn_shift
     )
-    back = mix_call(got, weight, partner, kept, local_weight, stat)
+    back = mix_call(got, partner, kept, z_forward, z_back, maps, stat, weight)
     back = lax.all_to_all(back.reshape(256, 1, 384), BOTH, 0, 0, tiled=True).reshape(768, 128)
     output = output_call(back, hidden, *rest)
     return output.reshape(16, 4, 16, 256)

time: 66.8 us -> 66.6 us (level)
  no operation moved by 1% of the time
where the time goes in v5:
time: 66.6 us; the launch traced here: 66.4 us
  starting transfers between devices  26.4 us (40%)
  blocking collectives  25.5 us (38%)
  Pallas kernels  12.4 us (19%)
  waiting for transfers between devices  2.04 us (3%)
    all_to_all x1, blocking collectives, on_device(): lax.all_to_all(back.reshape(256, 1, 384), BOTH, 0, 0, tiled=True)  25.5 us
    all_to_all x1, starting transfers between devices, on_device(): lax.all_to_all(sent.reshape(256, 2, 128), BOTH, 0, 0, tiled=True)  15.7 us
    ppermute x1, starting transfers between devices, on_device(): lax.ppermute(own, BOTH, [(16 * a, 16 * b) for a, b in zip(path[:-1], path...  10.7 us
    pallas_call x1, Pallas kernels, output_call(): pl.pallas_call(output_kernel, out_shape=pltpu.HBM((16, 64, 256), F32), in...  4.16 us
    pallas_call x1, Pallas kernels, forward_call(): pl.pallas_call(forward_kernel, out_shape=(pltpu.VMEM((512, 128), F32), pl...  3.05 us
    pallas_call x1, Pallas kernels, local_call(): pl.pallas_call(local_kernel, out_shape=(pltpu.VMEM((256, 128), F32), pltp...  2.66 us
    pallas_call x1, Pallas kernels, mix_call(): pl.pallas_call(mix_kernel, out_shape=pltpu.VMEM((768, 128), F32), in_spec...  2.53 us
    ppermute x1, waiting for transfers between devices, on_device(): lax.ppermute(own, BOTH, [(16 * a, 16 * b) for a, b in zip(path[:-1], path...  1.33 us
  transfers between devices with their start and end apart: 2, of which 2 were waited for; matrix products, arithmetic and copies ran while one was open for 0% of the time, Pallas kernels for 4%

profile of v5, /device:TPU:1, one launch (start us, length us, event | category | flops | bytes accessed | tf_op | source)
XLA Modules:
  0.0 66.4 jit_solution(7569654597834468000)
XLA Ops:
  0.0 3.1 %forward.1 = (f32[512,128]{1,0:T(8,128)}, f32[128,128]{1,0:T(8,128)S(1)}, f32[128,128]{1,0:T(8,128)S(1)}) custom-call(f32[2,512]{1,0:T(2,128)} %constant.10.clone.phase_hbm, f32[1024,256]{1,0:T(8,128)} %bitcast.17, f32[1024,32]{1,0:T(8,128)} %bitcast.19, bf16[256,256]{1,0:T(8,128)(2,1)} %constant.11.clone.y_hbm), custom_call_target="tpu_custom_call" | custom-call | flops 400000000 | bytes 4000000 | tf_op jit(solution)/shard_map/forward/pallas_call | solution.py:520
  3.1 15.7 %all-to-all-start = ((f32[256,2,128]{2,1,0:T(2,128)}), f32[256,2,128]{2,1,0:T(2,128)S(1)}, u32[]{:S(2)}, u32[]{:S(2)}) async-start(f32[256,2,128]{2,1,0:T(2,128)} %bitcast.3), calls=%async_computation | async-start | bytes 524288 | tf_op jit(solution)/shard_map/all_to_all | solution.py:623
  18.7 10.7 %collective-permute-start = (f32[128,128]{1,0:T(8,128)S(1)}, f32[128,128]{1,0:T(8,128)S(1)}, u32[]{:S(2)}, u32[]{:S(2)}) collective-permute-start(f32[128,128]{1,0:T(8,128)S(1)} %get-tuple-element.20), channel_id=1, source_target_pairs={{0,240},{240,16},{16,224},{224,32},{32,208},{208,48},{48,192},{192... | collective-permute-start | bytes 196616 | tf_op jit(solution)/shard_map/ppermute | solution.py:622
  29.4 2.7 %local.1 = (f32[256,128]{1,0:T(8,128)S(1)}, f32[128,64]{1,0:T(8,128)S(1)}, f32[16,16]{1,0:T(8,128)S(1)}, f32[1024,256]{1,0:T(8,128)S(1)}, f32[32,128]{1,0:T(8,12...) custom-call(f32[16,64,256]{2,1,0:T(8,128)} %bitcast.18, ...), custom_call_target="tpu_custom_call" | custom-call | flops 100000000 | bytes 2000000 | tf_op jit(solution)/shard_map/local/pallas_call | solution.py:545
  32.1 1.3 %collective-permute-done.partner_ref = f32[128,128]{1,0:T(8,128)S(1)} collective-permute-done((f32[128,128]{1,0:T(8,128)S(1)}, f32[128,128]{1,0:T(8,128)S(1)}, u32[]{:S(2)}, u32[]{:S(2)}) %collective-permute-start) | collective-permute-done | bytes 65568 | tf_op jit(solution)/shard_map/ppermute | solution.py:622
  33.4 0.7 %all-to-all-done = f32[256,2,128]{2,1,0:T(2,128)S(1)} async-done(((f32[256,2,128]{2,1,0:T(2,128)}), f32[256,2,128]{2,1,0:T(2,128)S(1)}, u32[]{:S(2)}, u32[]{:S(2)}) %all-to-all-start) | async-done | bytes 262176 | tf_op jit(solution)/shard_map/all_to_all | solution.py:623
  34.1 2.5 %mix.1 = f32[768,128]{1,0:T(8,128)S(1)} custom-call(f32[512,128]{1,0:T(8,128)S(1)} %bitcast.16, f32[128,128]{1,0:T(8,128)S(1)} %collective-permute-done.partner_ref, f32[128,128]{1,0:T(8,128)S(1)} %get-tuple-element.21.kept_ref, f32[256,128]{1,0:T(8,128)S(1)} %get-tuple-element.22.z_ref, f32[128,64]{1,0:T(8,128)S(1)} %get-tuple-element.23.back_ref, ...), custom_call_target="tpu_custom_call" | custom-call | flops 10000000 | bytes 1000000 | tf_op jit(solution)/shard_map/mix/pallas_call | solution.py:575
  36.7 25.5 %all_to_all.10 = f32[256,1,384]{2,1,0:T(1,128)S(1)} all-to-all(f32[256,1,384]{2,1,0:T(1,128)S(1)} %bitcast.15), channel_id=1, replica_groups=mesh['pa'=16,'pb'=16] {'pa','pb'}, dimensions={0} | all-to-all | bytes 786432 | tf_op jit(solution)/shard_map/all_to_all | solution.py:628
  62.2 4.2 %output.1 = f32[16,64,256]{2,1,0:T(8,128)} custom-call(f32[768,128]{1,0:T(8,128)S(1)} %bitcast.14, f32[1024,256]{1,0:T(8,128)S(1)} %get-tuple-element.26.hidden_ref, bf16[32,256]{1,0:T(8,128)(2,1)S(1)} %get-tuple-element.27.kan_ref, f32[16,128]{1,0:T(8,128)S(1)} %get-tuple-element.28.constant_ref, s32[2,1152,128]{2,1,0:T(8,128)S(1)} %get-tuple-element.29.index_ref, ...), custom_call_target="tpu_custom_call" | custom-call | flops 1000000000 | bytes 6000000 | tf_op jit(solution)/shard_map/output/pallas_call | solution.py:594
Async XLA Ops:
  3.1 31.1 %all-to-all-start = ((f32[256,2,128]{2,1,0:T(2,128)}), f32[256,2,128]{2,1,0:T(2,128)S(1)}, u32[]{:S(2)}, u32[]{:S(2)}) async-start(f32[256,2,128]{2,1,0:T(2,128)} %bitcast.3), calls=%async_computation | async-start | bytes 524288 | tf_op jit(solution)/shard_map/all_to_all | solution.py:623
  18.7 14.7 %collective-permute-start = (f32[128,128]{1,0:T(8,128)S(1)}, f32[128,128]{1,0:T(8,128)S(1)}, u32[]{:S(2)}, u32[]{:S(2)}) collective-permute-start(f32[128,128]{1,0:T(8,128)S(1)} %get-tuple-element.20), channel_id=1, source_target_pairs={{0,240},{240,16},{16,224},{224,32},{32,208},{208,48},{48,192},{192... | collective-permute-start | bytes 196616 | tf_op jit(solution)/shard_map/ppermute | solution.py:622

commit v6 on v5

--- a/solution.py
+++ b/solution.py
@@ -153,10 +153,13 @@
                     value, 64, axis=1
                 ) * (sign * phase_ref[1, index])
     copies[3].wait()
-    rows_ref[:, 0:32] = weight_ref[...]
-    for target, wanted in ((sent_ref, jnp.where(pa < 8, 1, 0)), (kept_ref, 0)):
-        chosen = rows_ref[pl.ds(wanted, 512, stride=2), :]
-        target[...] = jnp.concatenate([chosen[128 * q : 128 * (q + 1), 0:32] for q in range(4)], axis=1)
+
+    @pl.when(pb == 0)
+    def _():
+        rows_ref[:, 0:32] = weight_ref[...]
+        for target, wanted in ((sent_ref, jnp.where(pa < 8, 1, 0)), (kept_ref, 0)):
+            chosen = rows_ref[pl.ds(wanted, 512, stride=2), :]
+            target[...] = jnp.concatenate([chosen[128 * q : 128 * (q + 1), 0:32] for q in range(4)], axis=1)
 
 
 def local_kernel(

time: 66.6 us -> 66.6 us (level)
  no operation moved by 1% of the time
where the time goes in v6:
time: 66.6 us; the launch traced here: 66.4 us
  starting transfers between devices  26.1 us (39%)
  blocking collectives  25.5 us (38%)
  Pallas kernels  12.7 us (19%)
  waiting for transfers between devices  2.04 us (3%)
    all_to_all x1, blocking collectives, on_device(): lax.all_to_all(back.reshape(256, 1, 384), BOTH, 0, 0, tiled=True)  25.5 us
    all_to_all x1, starting transfers between devices, on_device(): lax.all_to_all(sent.reshape(256, 2, 128), BOTH, 0, 0, tiled=True)  15.4 us
    ppermute x1, starting transfers between devices, on_device(): lax.ppermute(own, BOTH, [(16 * a, 16 * b) for a, b in zip(path[:-1], path...  10.7 us
    pallas_call x1, Pallas kernels, output_call(): pl.pallas_call(output_kernel, out_shape=pltpu.HBM((16, 64, 256), F32), in...  4.16 us
    pallas_call x1, Pallas kernels, forward_call(): pl.pallas_call(forward_kernel, out_shape=(pltpu.VMEM((512, 128), F32), pl...  3.3 us
    pallas_call x1, Pallas kernels, local_call(): pl.pallas_call(local_kernel, out_shape=(pltpu.VMEM((256, 128), F32), pltp...  2.66 us
    pallas_call x1, Pallas kernels, mix_call(): pl.pallas_call(mix_kernel, out_shape=pltpu.VMEM((768, 128), F32), in_spec...  2.53 us
    ppermute x1, waiting for transfers between devices, on_device(): lax.ppermute(own, BOTH, [(16 * a, 16 * b) for a, b in zip(path[:-1], path...  1.33 us
  transfers between devices with their start and end apart: 2, of which 2 were waited for; matrix products, arithmetic and copies ran while one was open for 0% of the time, Pallas kernels for 4%

profile of v6, /device:TPU:1, one launch (start us, length us, event | category | flops | bytes accessed | tf_op | source)
XLA Modules:
  0.0 66.4 jit_solution(11763897261035351103)
XLA Ops:
  0.0 3.3 %forward.1 = (f32[512,128]{1,0:T(8,128)}, f32[128,128]{1,0:T(8,128)S(1)}, f32[128,128]{1,0:T(8,128)S(1)}) custom-call(f32[2,512]{1,0:T(2,128)} %constant.10.clone.phase_hbm, f32[1024,256]{1,0:T(8,128)} %bitcast.17, f32[1024,32]{1,0:T(8,128)} %bitcast.19, bf16[256,256]{1,0:T(8,128)(2,1)} %constant.11.clone.y_hbm), custom_call_target="tpu_custom_call" | custom-call | flops 400000000 | bytes 4000000 | tf_op jit(solution)/shard_map/forward/pallas_call | solution.py:523
  3.3 15.4 %all-to-all-start = ((f32[256,2,128]{2,1,0:T(2,128)}), f32[256,2,128]{2,1,0:T(2,128)S(1)}, u32[]{:S(2)}, u32[]{:S(2)}) async-start(f32[256,2,128]{2,1,0:T(2,128)} %bitcast.3), calls=%async_computation | async-start | bytes 524288 | tf_op jit(solution)/shard_map/all_to_all | solution.py:626
  18.7 10.7 %collective-permute-start = (f32[128,128]{1,0:T(8,128)S(1)}, f32[128,128]{1,0:T(8,128)S(1)}, u32[]{:S(2)}, u32[]{:S(2)}) collective-permute-start(f32[128,128]{1,0:T(8,128)S(1)} %get-tuple-element.20), channel_id=1, source_target_pairs={{0,240},{240,16},{16,224},{224,32},{32,208},{208,48},{48,192},{192... | collective-permute-start | bytes 196616 | tf_op jit(solution)/shard_map/ppermute | solution.py:625
  29.4 2.7 %local.1 = (f32[256,128]{1,0:T(8,128)S(1)}, f32[128,64]{1,0:T(8,128)S(1)}, f32[16,16]{1,0:T(8,128)S(1)}, f32[1024,256]{1,0:T(8,128)S(1)}, f32[32,128]{1,0:T(8,12...) custom-call(f32[16,64,256]{2,1,0:T(8,128)} %bitcast.18, ...), custom_call_target="tpu_custom_call" | custom-call | flops 100000000 | bytes 2000000 | tf_op jit(solution)/shard_map/local/pallas_call | solution.py:548
  32.1 1.3 %collective-permute-done.partner_ref = f32[128,128]{1,0:T(8,128)S(1)} collective-permute-done((f32[128,128]{1,0:T(8,128)S(1)}, f32[128,128]{1,0:T(8,128)S(1)}, u32[]{:S(2)}, u32[]{:S(2)}) %collective-permute-start) | collective-permute-done | bytes 65568 | tf_op jit(solution)/shard_map/ppermute | solution.py:625
  33.4 0.7 %all-to-all-done = f32[256,2,128]{2,1,0:T(2,128)S(1)} async-done(((f32[256,2,128]{2,1,0:T(2,128)}), f32[256,2,128]{2,1,0:T(2,128)S(1)}, u32[]{:S(2)}, u32[]{:S(2)}) %all-to-all-start) | async-done | bytes 262176 | tf_op jit(solution)/shard_map/all_to_all | solution.py:626
  34.1 2.5 %mix.1 = f32[768,128]{1,0:T(8,128)S(1)} custom-call(f32[512,128]{1,0:T(8,128)S(1)} %bitcast.16, f32[128,128]{1,0:T(8,128)S(1)} %collective-permute-done.partner_ref, f32[128,128]{1,0:T(8,128)S(1)} %get-tuple-element.21.kept_ref, f32[256,128]{1,0:T(8,128)S(1)} %get-tuple-element.22.z_ref, f32[128,64]{1,0:T(8,128)S(1)} %get-tuple-element.23.back_ref, ...), custom_call_target="tpu_custom_call" | custom-call | flops 10000000 | bytes 1000000 | tf_op jit(solution)/shard_map/mix/pallas_call | solution.py:578
  36.7 25.5 %all_to_all.10 = f32[256,1,384]{2,1,0:T(1,128)S(1)} all-to-all(f32[256,1,384]{2,1,0:T(1,128)S(1)} %bitcast.15), channel_id=1, replica_groups=mesh['pa'=16,'pb'=16] {'pa','pb'}, dimensions={0} | all-to-all | bytes 786432 | tf_op jit(solution)/shard_map/all_to_all | solution.py:631
  62.2 4.2 %output.1 = f32[16,64,256]{2,1,0:T(8,128)} custom-call(f32[768,128]{1,0:T(8,128)S(1)} %bitcast.14, f32[1024,256]{1,0:T(8,128)S(1)} %get-tuple-element.26.hidden_ref, bf16[32,256]{1,0:T(8,128)(2,1)S(1)} %get-tuple-element.27.kan_ref, f32[16,128]{1,0:T(8,128)S(1)} %get-tuple-element.28.constant_ref, s32[2,1152,128]{2,1,0:T(8,128)S(1)} %get-tuple-element.29.index_ref, ...), custom_call_target="tpu_custom_call" | custom-call | flops 1000000000 | bytes 6000000 | tf_op jit(solution)/shard_map/output/pallas_call | solution.py:597
Async XLA Ops:
  3.3 30.8 %all-to-all-start = ((f32[256,2,128]{2,1,0:T(2,128)}), f32[256,2,128]{2,1,0:T(2,128)S(1)}, u32[]{:S(2)}, u32[]{:S(2)}) async-start(f32[256,2,128]{2,1,0:T(2,128)} %bitcast.3), calls=%async_computation | async-start | bytes 524288 | tf_op jit(solution)/shard_map/all_to_all | solution.py:626
  18.7 14.7 %collective-permute-start = (f32[128,128]{1,0:T(8,128)S(1)}, f32[128,128]{1,0:T(8,128)S(1)}, u32[]{:S(2)}, u32[]{:S(2)}) collective-permute-start(f32[128,128]{1,0:T(8,128)S(1)} %get-tuple-element.20), channel_id=1, source_target_pairs={{0,240},{240,16},{16,224},{224,32},{32,208},{208,48},{48,192},{192... | collective-permute-start | bytes 196616 | tf_op jit(solution)/shard_map/ppermute | solution.py:625
